TPU v7x, 32 devices: a whole 2x2x4 slice. The times are simulated.
32 devices in a mesh: outer: 8 (over z, core), inner: 4 (over y, x).
Axes of the slice: x: 2, y: 2, z: 4, core: 2. Of those that a mesh axis runs over, the one named last changes fastest.
Arguments:
- queries: bfloat16 [4096, 4096], P(('outer', 'inner')), may hold values from -8 to 8
- keys: bfloat16 [4096, 512], P(('outer', 'inner')), may hold values from -8 to 8
- values: bfloat16 [4096, 512], P(('outer', 'inner')), may hold values from -6 to 6
- acc_out: bfloat16 [4096, 4096], P(('outer', 'inner')), may hold values from -6 to 6
- acc_max: float32 [4096, 32], P(('outer', 'inner')), may hold values from 2 to 4
- acc_sum: float32 [4096, 32], P(('outer', 'inner')), may hold values from 16 to 256
- doc_lengths: int32 [16], replicated, may hold values from 1 to 2048, as said below
Outputs:
- new_out: bfloat16 [4096, 4096], P(('outer', 'inner'))
- new_max: float32 [4096, 32], P(('outer', 'inner'))
- new_sum: float32 [4096, 32], P(('outer', 'inner'))
Inputs may be any that keep to these rules, and one draw needn't show every extreme that they name: `doc_lengths`: the lengths add up to 4096; one document is exactly 2048 long and none is longer.
All inputs are finite; a program needn't handle non-finite values.
Results may differ from a plain program's by a relative error of at most 0.0014.
Values may be sent and summed in bfloat16 or wider, within the bound.
No kernel may reach another device: no remote copies, remote signals or barrier semaphores. Data moves between devices by JAX's collectives and lax.ppermute only.
A program may use at most 64 MiB of HBM per device.

v0:
```python
import math

import jax
import jax.numpy as jnp
from jax import lax
from jax.sharding import PartitionSpec as P

HD = 128


NEG = -1e30


def shifted(value, axis, steps):
    count = lax.axis_size(axis)
    initial, last = (max(0, -steps), min(count, count - steps))
    return lax.ppermute(value, axis, [(source, source + steps) for source in range(initial, last)])


def doc_start_of(doc_lengths, positions):
    ends = jnp.cumsum(doc_lengths)
    starts = ends - doc_lengths
    inside = starts[None, :] <= positions[:, None]
    return jnp.max(jnp.where(inside, starts[None, :], 0), axis=1)


def attend_block(carry, q_heads, key_tile, value_tile, kpos, qpos, qstart, scale):
    mask = (kpos[None, :] <= qpos[:, None]) & (kpos[None, :] >= qstart[:, None])

    def live(state):
        run_max, run_sum, run_out = state
        scores = (
            jnp.einsum("rhgd,nhd->rhgn", q_heads, key_tile, preferred_element_type=jnp.float32)
            * scale
        )
        keep = mask[:, None, None, :]
        scores = jnp.where(keep, scores, NEG)
        top = jnp.maximum(run_max, jnp.max(scores, axis=-1))
        shrink = jnp.exp(run_max - top)
        weights = jnp.where(keep, jnp.exp(scores - top[..., None]), 0.0)
        total = run_sum * shrink + jnp.sum(weights, axis=-1)
        mixed = jnp.einsum(
            "rhgn,nhd->rhgd",
            weights.astype(jnp.bfloat16),
            value_tile,
            preferred_element_type=jnp.float32,
        )
        return (top, total, run_out * shrink[..., None] + mixed)

    return lax.cond(jnp.any(mask), live, lambda state: state, carry)


def body(queries, keys, values, acc_out, acc_max, acc_sum, doc_lengths):
    rows = queries.shape[0]
    heads = acc_max.shape[1]
    kv_heads = keys.shape[1] // HD
    group = heads // kv_heads
    n_outer = lax.axis_size("outer")
    n_inner = lax.axis_size("inner")
    block = rows * n_inner
    outer_at = lax.axis_index("outer")
    inner_at = lax.axis_index("inner")
    scale = 1.0 / math.sqrt(HD)
    k_block = (outer_at + n_outer - 1) % n_outer
    key_here, value_here = shifted((keys, values), "outer", 1)
    qpos = outer_at * block + inner_at * rows + jnp.arange(rows, dtype=jnp.int32)
    qstart = doc_start_of(doc_lengths, qpos)
    q_heads = queries.reshape(rows, kv_heads, group, HD)
    start_state = (
        jnp.full((rows, kv_heads, group), NEG, jnp.float32),
        jnp.zeros((rows, kv_heads, group), jnp.float32),
        jnp.zeros((rows, kv_heads, group, HD), jnp.float32),
    )
    carry = start_state
    key_rows = lax.all_gather(key_here, "inner", axis=0, tiled=True)
    value_rows = lax.all_gather(value_here, "inner", axis=0, tiled=True)
    count = key_rows.shape[0]
    width = 512
    number = count // width
    key_tiles = key_rows.reshape(number, width, kv_heads, HD)
    value_tiles = value_rows.reshape(number, width, kv_heads, HD)
    offsets = width * jnp.arange(number, dtype=jnp.int32)

    def one_tile(state, item):
        key_tile, value_tile, first = item
        kpos = k_block * block + first + jnp.arange(width, dtype=jnp.int32)
        return (attend_block(state, q_heads, key_tile, value_tile, kpos, qpos, qstart, scale), None)

    carry, unused = lax.scan(one_tile, carry, (key_tiles, value_tiles, offsets))
    part_max, part_sum, part_out = carry
    old_max = acc_max.reshape(rows, kv_heads, group)
    old_sum = acc_sum.reshape(rows, kv_heads, group)
    top = jnp.maximum(old_max, part_max)
    kept = old_sum * jnp.exp(old_max - top)
    fresh = jnp.exp(part_max - top)
    total = kept + part_sum * fresh
    old_out = acc_out.reshape(rows, kv_heads, group, HD).astype(jnp.float32)
    result = (old_out * kept[..., None] + part_out * fresh[..., None]) / total[..., None]
    return (
        result.reshape(rows, heads * HD).astype(jnp.bfloat16),
        top.reshape(rows, heads),
        total.reshape(rows, heads),
    )


def solution(mesh):
    return jax.shard_map(
        body,
        mesh=mesh,
        in_specs=(
            P(("outer", "inner"), None),
            P(("outer", "inner"), None),
            P(("outer", "inner"), None),
            P(("outer", "inner"), None),
            P(("outer", "inner"), None),
            P(("outer", "inner"), None),
            P(),
        ),
        out_specs=(
            P(("outer", "inner"), None),
            P(("outer", "inner"), None),
            P(("outer", "inner"), None),
        ),
        check_vma=False,
    )
```

profile of v0, /device:TPU:8, one launch (start us, length us, event | category | flops | bytes accessed | tf_op | source)
XLA Modules:
  0.0 60.2 jit_solution(4065774480520654403)
XLA Ops:
  0.6 1.9 %collective-permute-start = (bf16[128,512]{1,0:T(8,128)(2,1)}, bf16[128,512]{1,0:T(8,128)(2,1)S(1)}, u32[]{:S(2)}, u32[]{:S(2)}) collective-permute-start(bf16[128,512]{1,0:T(8,128)(2,1)} %param.10), channel_id=1, source_target_pairs={{0,4},{4,8},{8,12},{12,16},{16,20},{20,24},{24,28},{1,5},{5,9},{9,... | collective-permute-start | bytes 393224 | tf_op jit(solution)/shard_map/ppermute | solution.py:17
  2.6 3.6 %collective-permute-start.1 = (bf16[128,512]{1,0:T(8,128)(2,1)}, bf16[128,512]{1,0:T(8,128)(2,1)S(1)}, u32[]{:S(2)}, u32[]{:S(2)}) collective-permute-start(bf16[128,512]{1,0:T(8,128)(2,1)} %param.11), channel_id=1, source_target_pairs={{0,4},{4,8},{8,12},{12,16},{16,20},{20,24},{24,28},{1,5},{5,9},{9,... | collective-permute-start | bytes 393224 | tf_op jit(solution)/shard_map/ppermute | solution.py:17
  6.2 0.7 %copy.30 = s32[16,1]{1,0:T(8,128)S(1)} copy(s32[16,1]{0,1:T(1,128)} %bitcast.52) | data formatting | bytes 128 | tf_op jit(solution)/shard_map/reshape.49
  7.0 0.1 reduce
  7.1 0.7 %sub.24 = s32[16]{0:T(128)S(1)} subtract(s32[16]{0:T(128)S(1)} %reduce, s32[16]{0:T(128)} %param.15) | non-fusion elementwise | flops 16 | bytes 192 | tf_op jit(solution)/shard_map/sub | solution.py:22
  7.7 0.1 select_reduce_fusion
  7.8 0.8 %compare_and_fusion = (pred[128,512]{0,1:T(8,128)(4,1)S(1)}, pred[]{:T(512)}) fusion(s32[128]{0:T(128)S(1)} %select_reduce_fusion, s32[128]{0:T(128)S(1)} %iota_add_fusion.1, s32[512]{0:T(512)S(1)} %iota_add_fusion), kind=kLoop, calls=%fused_computation.21 | loop fusion | flops 262143 | bytes 68609 | tf_op jit(solution)/shard_map/while/body/eval_jaxpr/and | solution.py:28
  9.3 2.3 %copy.29 = bf16[128,4096]{0,1:T(8,128)(2,1)} copy(bf16[128,4096]{1,0:T(8,128)(2,1)} %param.12) | data formatting | bytes 2097152 | tf_op args[3]
  11.5 0.2 broadcast_in_dim.56
  11.8 0.0 collective-permute-done
  11.8 11.0 %all_gather.6 = bf16[512,512]{1,0:T(8,128)(2,1)} all-gather(bf16[128,512]{1,0:T(8,128)(2,1)S(1)} %collective-permute-done), channel_id=1, replica_groups=mesh['outer'=8,'inner'=4] {'inner'}, dimensions={0}, use_global_device_ids=true | all-gather | bytes 655360 | tf_op jit(solution)/shard_map/all_gather | solution.py:75
  22.8 0.0 collective-permute-done.1
  22.8 10.7 %all_gather.7 = bf16[512,512]{1,0:T(8,128)(2,1)} all-gather(bf16[128,512]{1,0:T(8,128)(2,1)S(1)} %collective-permute-done.1), channel_id=1, replica_groups=mesh['outer'=8,'inner'=4] {'inner'}, dimensions={0}, use_global_device_ids=true | all-gather | bytes 655360 | tf_op jit(solution)/shard_map/all_gather | solution.py:76
  33.5 0.0 copy-start.3
  33.5 0.0 copy-start.4
  33.5 22.4 %conditional.1 = (f32[128,4,8]{0,2,1:T(8,128)S(1)}, f32[128,4,8]{0,2,1:T(8,128)S(1)}, f32[128,4,8,128]{0,3,2,1:T(8,128)}) conditional(s32[]{:T(128)} %convert_element_type.21, (f32[128,4,8]{0,2,1:T(8,128)S(1)}, f32[128,4,8]{0,2,1:T(8,128)S(1)}, f32[128,4,8,128]{3,0,2,1:T(8,128)S(1)}) %tuple.17, (pred[128,512]{0,1:T(8,128)(4,1)S(1)}, ...), branch_computations={%region_3.4_spmd, %region_4.7_spmd} | conditional | flops 1102061568 | bytes 75956304 | solution.py:50
  33.5 1.4 %copy.42 = bf16[16,8,32,128]{3,2,1,0:T(8,128)(2,1)S(1)} copy(bf16[16,8,32,128]{3,1,2,0:T(8,128)(2,1)} %bitcast.49) | data formatting | bytes 2097152 | tf_op jit(solution)/shard_map/while/body/eval_jaxpr/cond
  35.0 2.0 %squeeze.12 = bf16[512,4,128]{2,1,0:T(4,128)(2,1)} reshape(bf16[512,512]{1,0:T(8,128)(2,1)} %get-tuple-element.45) | data formatting | bytes 1048576 | tf_op jit(solution)/shard_map/while/body/jit(dynamic_index_in_dim)/squeeze | solution.py:89
  36.9 2.8 %fusion = (f32[128,4,8]{0,2,1:T(8,128)S(1)}, f32[4,512,128,8]{2,1,3,0:T(8,128)S(1)}) fusion(pred[128,512]{0,1:T(8,128)(4,1)S(1)} %get-tuple-element.44, bf16[128,4,8,128]{3,2,1,0:T(8,128)(2,1)S(1)} %bitcast.45, bf16[512,4,128,1]{2,1,0,3:T(4,128)(2,1)} %bitcast.48), kind=kOutput, calls=%fused_computation.2 | convolution fusion | flops 543158272 | bytes 10043392 | tf_op jit(solution)/shard_map/while/body/eval_jaxpr/cond/branch_1_fun/rhgd,nhd->rhgn/dot_general | solution.py:33
  39.7 0.0 copy-start
  39.7 0.0 copy-start.1
  39.7 3.2 %copy-done = f32[4,512,128,8]{2,1,3,0:T(8,128)} copy-done((f32[4,512,128,8]{2,1,3,0:T(8,128)}, f32[4,512,128,8]{2,1,3,0:T(8,128)S(1)}, u32[]{:S(2)}) %copy-start) | copy-done | bytes 8388632 | tf_op jit(solution)/shard_map/while/body/eval_jaxpr/cond
  42.9 2.1 %fusion.2 = f32[128,4,8]{0,2,1:T(8,128)S(1)} fusion(f32[4,512,128,8]{2,1,3,0:T(8,128)S(1)} %get-tuple-element.87, f32[128,4,8]{0,2,1:T(8,128)S(1)} %max.4, pred[128,512]{0,1:T(8,128)(4,1)S(1)} %get-tuple-element.44), kind=kLoop, calls=%fused_computation.4 | loop fusion | flops 10481664 | bytes 8486912 | tf_op jit(solution)/shard_map/while/body/eval_jaxpr/cond/branch_1_fun/reduce_sum | solution.py:41
  45.1 0.0 copy-done.1
  45.1 0.1 squeeze.13
  45.2 7.7 %bitcast_add_fusion = f32[128,4,8,128]{3,0,2,1:T(8,128)} fusion(f32[128,4,8,128]{3,0,2,1:T(8,128)S(1)} %get-tuple-element.48, f32[4,512,128,8]{2,1,3,0:T(8,128)} %copy-done, f32[128,4,8]{0,2,1:T(8,128)S(1)} %max.4, pred[128,512]{0,1:T(8,128)(4,1)S(1)} %get-tuple-element.44, f32[128,4,8]{0,2,1:T(8,128)S(1)} %get-tuple-element.82, ...), kind=kOutput, calls=%fused_computation.7 | convolution fusion | flops 548405248 | bytes 13205504 | tf_op jit(solution)/shard_map/while/body/eval_jaxpr/cond/branch_1_fun/rhgn,nhd->rhgd/dot_general | solution.py:42
  52.9 2.9 %copy.41 = f32[128,4,8,128]{0,3,2,1:T(8,128)} copy(f32[128,4,8,128]{3,0,2,1:T(8,128)} %bitcast_add_fusion) | data formatting | bytes 4194304 | tf_op jit(solution)/shard_map/while/body/eval_jaxpr/cond | solution.py:50
  55.8 0.0 copy-done.3
  55.8 0.0 copy-done.4
  55.8 0.6 %multiply_add_fusion.1 = (f32[128,4,8]{0,2,1:T(8,128)S(1)}, f32[128,4,8]{0,2,1:T(8,128)S(1)}, f32[128,4,8]{0,2,1:T(8,128)S(1)}, f32[128,32]{0,1:T(8,128)}) fusion(f32[128,4,8]{0,2,1:T(8,128)S(1)} %get-tuple-element.68, f32[128,4,8]{0,2,1:T(8,128)S(1)} %get-tuple-element.66, f32[128,32]{0,1:T(8,128)S(1)} %copy-done.3, f32[128,32]{0,1:T(8,128)S(1)} %copy-done.4), kind=kLoop, calls=%fused_computation.26 | loop fusion | flops 24576 | bytes 131072 | tf_op jit(solution)/shard_map/add | solution.py:96
  56.5 0.0 copy-start.2
  56.5 2.4 %fusion.17 = bf16[128,4,8,128]{0,3,2,1:T(8,128)(2,1)S(1)} fusion(bf16[128,4,8,128]{0,3,2,1:T(8,128)(2,1)} %bitcast.46, f32[128,4,8,128]{0,3,2,1:T(8,128)} %get-tuple-element.80, f32[128,4,8]{0,2,1:T(8,128)S(1)} %get-tuple-element.83, f32[128,4,8]{0,2,1:T(8,128)S(1)} %get-tuple-element.84, f32[128,4,8]{0,2,1:T(8,128)S(1)} %get-tuple-element.85), kind=kLoop, calls=%fused_computation.20 | loop fusion | flops 3145728 | bytes 4243456 | tf_op jit(solution)/shard_map/convert_element_type | solution.py:100
  58.9 1.3 %copy.32 = bf16[128,4096]{1,0:T(8,128)(2,1)} copy(bf16[128,4096]{0,1:T(8,128)(2,1)S(1)} %bitcast.47) | data formatting | bytes 2097152
  60.2 0.0 copy-done.2
  (8 shorter events, 0.1 us)
Async XLA Ops:
  0.6 11.2 %collective-permute-start = (bf16[128,512]{1,0:T(8,128)(2,1)}, bf16[128,512]{1,0:T(8,128)(2,1)S(1)}, u32[]{:S(2)}, u32[]{:S(2)}) collective-permute-start(bf16[128,512]{1,0:T(8,128)(2,1)} %param.10), channel_id=1, source_target_pairs={{0,4},{4,8},{8,12},{12,16},{16,20},{20,24},{24,28},{1,5},{5,9},{9,... | collective-permute-start | bytes 393224 | tf_op jit(solution)/shard_map/ppermute | solution.py:17
  2.6 20.2 %collective-permute-start.1 = (bf16[128,512]{1,0:T(8,128)(2,1)}, bf16[128,512]{1,0:T(8,128)(2,1)S(1)}, u32[]{:S(2)}, u32[]{:S(2)}) collective-permute-start(bf16[128,512]{1,0:T(8,128)(2,1)} %param.11), channel_id=1, source_target_pairs={{0,4},{4,8},{8,12},{12,16},{16,20},{20,24},{24,28},{1,5},{5,9},{9,... | collective-permute-start | bytes 393224 | tf_op jit(solution)/shard_map/ppermute | solution.py:17
  33.5 22.4 %copy-start.3 = (f32[128,32]{0,1:T(8,128)S(1)}, f32[128,32]{0,1:T(8,128)}, u32[]{:S(2)}) copy-start(f32[128,32]{0,1:T(8,128)} %param.13) | copy-start | bytes 49156
  33.5 22.4 %copy-start.4 = (f32[128,32]{0,1:T(8,128)S(1)}, f32[128,32]{0,1:T(8,128)}, u32[]{:S(2)}) copy-start(f32[128,32]{0,1:T(8,128)} %param.14) | copy-start | bytes 49156
  39.7 3.2 %copy-start = (f32[4,512,128,8]{2,1,3,0:T(8,128)}, f32[4,512,128,8]{2,1,3,0:T(8,128)S(1)}, u32[]{:S(2)}) copy-start(f32[4,512,128,8]{2,1,3,0:T(8,128)S(1)} %get-tuple-element.87) | copy-start | bytes 25165828 | tf_op jit(solution)/shard_map/while/body/eval_jaxpr/cond
  39.7 5.4 %copy-start.1 = (bf16[512,512]{1,0:T(8,128)(2,1)S(1)}, bf16[512,512]{1,0:T(8,128)(2,1)}, u32[]{:S(2)}) copy-start(bf16[512,512]{1,0:T(8,128)(2,1)} %get-tuple-element.49) | copy-start | bytes 1572868 | tf_op jit(solution)/shard_map/while/body/eval_jaxpr/cond
  56.5 3.8 %copy-start.2 = (f32[128,4,8]{0,2,1:T(8,128)}, f32[128,4,8]{0,2,1:T(8,128)S(1)}, u32[]{:S(2)}) copy-start(f32[128,4,8]{0,2,1:T(8,128)S(1)} %get-tuple-element.83) | copy-start | bytes 49156
where the time goes:
time: 60.6 us; the launch traced here: 60.2 us
  blocking collectives  21.7 us (36%)
  local copies, waits for them, and re-layouts  14.2 us (23%)
  matrix products  10.4 us (17%)
  other arithmetic  6.9 us (11%)
  starting transfers between devices  5.51 us (9%)
  between operations  1.39 us (2%)
    all_gather x1, blocking collectives, body(): key_rows = lax.all_gather(key_here, 'inner', axis=0, tiled=True)  11 us
    all_gather x1, blocking collectives, body(): value_rows = lax.all_gather(value_here, 'inner', axis=0, tiled=True)  10.7 us
    dot_general x1, matrix products, live(): jnp.einsum('rhgn,nhd->rhgd', weights.astype(jnp.bfloat16), value_tile, pr...  7.66 us
    ppermute x2, starting transfers between devices, shifted(): lax.ppermute(value, axis, [(source, source + steps) for source in range(i...  5.51 us
    cond x6, local copies, waits for them, and re-layouts  4.64 us
    unnamed x8, local copies, waits for them, and re-layouts  3.59 us
    cond x1, local copies, waits for them, and re-layouts, attend_block(): return lax.cond(jnp.any(mask), live, lambda state: state, carry)  2.94 us
    dot_general x1, matrix products, live(): jnp.einsum('rhgd,nhd->rhgn', q_heads, key_tile, preferred_element_type=jn...  2.77 us
  transfers between devices with their start and end apart: 2, of which 0 were waited for; matrix products, arithmetic and copies ran while one was open for 8% of the time, Pallas kernels for 0%

commit v1 on v0

v1 whole, which is shorter than its diff:
```python
import functools
import math

import jax
import jax.numpy as jnp
from jax import lax
from jax.experimental import pallas as pl
from jax.experimental.pallas import tpu as pltpu
from jax.sharding import PartitionSpec as P

HD = 128
LANES = 128
HIDE = -1e30
LOG2E = math.log2(math.e)


def mask_kernel(block, docs, doc_ref, mine_ref, hide_ref):
    rows = mine_ref.shape[0]
    outer_at = lax.axis_index("outer")
    inner_at = lax.axis_index("inner")
    lane = lax.broadcasted_iota(jnp.int32, (8, LANES), 1)
    far = jnp.full((8, LANES), 2**30, jnp.int32)

    def one(d, state):
        first, starts, ends = state
        last = first + doc_ref[d]
        return last, jnp.where(lane == d, first, starts), jnp.where(lane == d, last, ends)

    unused, starts, ends = lax.fori_loop(0, docs, one, (jnp.int32(0), far, far))
    starts, ends = starts[:1], ends[:1]
    tok = lax.broadcasted_iota(jnp.int32, (rows, LANES), 0)
    qpos = tok + (outer_at * block + inner_at * rows)
    mine_ref[...] = jnp.where((starts <= qpos) & (qpos < ends), 1.0, 0.0).astype(jnp.bfloat16)
    for step in range(hide_ref.shape[0]):
        kpos = tok + ((outer_at - 1) * block + (inner_at ^ step) * rows)
        hide_ref[step] = jnp.where(kpos < starts, HIDE, 0.0).astype(jnp.bfloat16)


def attend_kernel(parts, kv_heads, group, scale, *refs):
    q_ref, old_ref, max_ref, sum_ref, mine_ref, hide_ref = refs[:6]
    kv_refs = refs[6 : 6 + parts]
    out_ref, new_max_ref, new_sum_ref, stage, sems = refs[6 + parts :]
    rows = q_ref.shape[0]
    heads = kv_heads * group
    wide = group * HD
    lane = lax.broadcasted_iota(jnp.int32, (rows, heads), 1)
    mine = mine_ref[...]
    ones = jnp.ones((parts * rows, HD), jnp.bfloat16)

    def one(h, unused):
        cols = pl.ds(pl.multiple_of(h * HD, HD), HD)
        vcols = pl.ds(pl.multiple_of((h + kv_heads) * HD, HD), HD)
        keys = jnp.concatenate(
            [jnp.concatenate([kv[:, cols], hide_ref[j]], axis=1) for j, kv in enumerate(kv_refs)], axis=0
        )
        vals = jnp.concatenate([jnp.concatenate([kv[:, vcols] for kv in kv_refs], axis=0), ones], axis=1)
        for g in range(group):
            head = h * group + g
            at = pl.ds(pl.multiple_of(head * HD, HD), HD)
            q = jnp.concatenate([q_ref[:, at], mine], axis=1)
            s = lax.dot_general(q, keys, (((1,), (1,)), ((), ())), preferred_element_type=jnp.float32)
            old_max = jnp.sum(jnp.where(lane == head, max_ref[...], 0.0), axis=1, keepdims=True)
            old_sum = jnp.sum(jnp.where(lane == head, sum_ref[...], 0.0), axis=1, keepdims=True)
            top = jnp.maximum(old_max, jnp.max(s, axis=1, keepdims=True) * scale)
            w = jnp.exp2(s * (scale * LOG2E) - top * LOG2E).astype(jnp.bfloat16)
            mixed = jnp.dot(w, vals, preferred_element_type=jnp.float32)
            kept = old_sum * jnp.exp2((old_max - top) * LOG2E)
            total = mixed[:, HD:] + kept
            result = (old_ref[:, at].astype(jnp.float32) * kept + mixed[:, :HD]) / total
            stage[:, at] = result.astype(jnp.bfloat16)
            new_max_ref[...] = jnp.where(lane == head, top, new_max_ref[...])
            new_sum_ref[...] = jnp.where(lane == head, total[:, :heads], new_sum_ref[...])
        span = pl.ds(pl.multiple_of(h * wide, wide), wide)
        pltpu.make_async_copy(stage.at[:, span], out_ref.at[:, span], sems.at[h]).start()
        return unused

    lax.fori_loop(0, kv_heads, one, 0)
    for h in range(kv_heads):
        span = pl.ds(h * wide, wide)
        pltpu.make_async_copy(stage.at[:, span], out_ref.at[:, span], sems.at[h]).wait()


def body(queries, keys, values, acc_out, acc_max, acc_sum, doc_lengths):
    rows = queries.shape[0]
    heads = acc_max.shape[1]
    kv_heads = keys.shape[1] // HD
    group = heads // kv_heads
    n_outer = lax.axis_size("outer")
    n_inner = lax.axis_size("inner")
    docs = doc_lengths.shape[0]
    vmem = pl.BlockSpec(memory_space=pltpu.VMEM)
    mine, hide = pl.pallas_call(
        functools.partial(mask_kernel, rows * n_inner, docs),
        out_shape=(
            jax.ShapeDtypeStruct((rows, LANES), jnp.bfloat16),
            jax.ShapeDtypeStruct((n_inner, rows, LANES), jnp.bfloat16),
        ),
        in_specs=[pl.BlockSpec(memory_space=pltpu.SMEM)],
        out_specs=(vmem, vmem),
    )(doc_lengths)
    both = jnp.concatenate([keys, values], axis=1)
    got = []
    for step in range(n_inner):
        pairs = [
            (o * n_inner + i, (o + 1) % n_outer * n_inner + (i ^ step))
            for o in range(n_outer)
            for i in range(n_inner)
        ]
        got.append(lax.ppermute(both, ("outer", "inner"), pairs))
    flops = 4 * rows * n_inner * rows * heads * HD
    return pl.pallas_call(
        functools.partial(attend_kernel, n_inner, kv_heads, group, 1.0 / math.sqrt(HD)),
        out_shape=(
            jax.ShapeDtypeStruct(queries.shape, jnp.bfloat16),
            jax.ShapeDtypeStruct((rows, heads), jnp.float32),
            jax.ShapeDtypeStruct((rows, heads), jnp.float32),
        ),
        in_specs=[vmem] * (6 + n_inner),
        out_specs=(pl.BlockSpec(memory_space=pl.ANY), vmem, vmem),
        scratch_shapes=[pltpu.VMEM(queries.shape, jnp.bfloat16), pltpu.SemaphoreType.DMA((kv_heads,))],
        compiler_params=pltpu.CompilerParams(vmem_limit_bytes=32 * 2**20),
        cost_estimate=pl.CostEstimate(flops=flops, bytes_accessed=4 * 2**20, transcendentals=0),
    )(queries, acc_out, acc_max, acc_sum, mine, hide, *got)


def solution(mesh):
    split = P(("outer", "inner"), None)
    return jax.shard_map(
        body,
        mesh=mesh,
        in_specs=(split,) * 6 + (P(),),
        out_specs=(split,) * 3,
        check_vma=False,
    )
```

time: 60.6 us -> 38.9 us (0.64)
  the two profiles are of different devices: /device:TPU:8 before, /device:TPU:0 now
where the time goes in v1:
time: 38.9 us; the launch traced here: 38.6 us
  Pallas kernels  13.4 us (34%)
  waiting for transfers between devices  11 us (28%)
  starting transfers between devices  6.85 us (18%)
  local copies, waits for them, and re-layouts  6.64 us (17%)
  between operations  0.69 us (2%)
    pallas_call x1, Pallas kernels, body(): pl.pallas_call(functools.partial(attend_kernel, n_inner, kv_heads, group,...  11.9 us
    ppermute x4, waiting for transfers between devices, body(): got.append(lax.ppermute(both, ('outer', 'inner'), pairs))  11 us
    ppermute x4, starting transfers between devices, body(): got.append(lax.ppermute(both, ('outer', 'inner'), pairs))  6.85 us
    unnamed x17, local copies, waits for them, and re-layouts  5.27 us
    pallas_call x1, Pallas kernels, body(): pl.pallas_call(functools.partial(mask_kernel, rows * n_inner, docs), out_...  1.48 us
    pallas_call x2, local copies, waits for them, and re-layouts, body(): pl.pallas_call(functools.partial(attend_kernel, n_inner, kv_heads, group,...  1.36 us
  transfers between devices with their start and end apart: 4, of which 4 were waited for; matrix products, arithmetic and copies ran while one was open for 0% of the time, Pallas kernels for 4%

profile of v1, /device:TPU:0, one launch (start us, length us, event | category | flops | bytes accessed | tf_op | source)
XLA Modules:
  0.0 38.6 jit_solution(18322335981704475964)
XLA Ops:
  0.6 0.0 copy-start.4
  0.6 0.9 %constant_dynamic-update-slice_fusion.1 = bf16[128,1024]{1,0:T(8,128)(2,1)S(1)} fusion(bf16[128,512]{1,0:T(8,128)(2,1)} %param.8), kind=kLoop, calls=%fused_computation.1 | loop fusion | bytes 262144
  1.6 0.0 copy-done.4
  1.6 0.0 copy-start.5
  1.6 0.0 copy-start.6
  1.6 3.4 %collective-permute-start.3 = (bf16[128,1024]{1,0:T(8,128)(2,1)S(1)}, bf16[128,1024]{1,0:T(8,128)(2,1)S(1)}, u32[]{:S(2)}, u32[]{:S(2)}) collective-permute-start(bf16[128,1024]{1,0:T(8,128)(2,1)S(1)} %constant_dynamic-update-slice_fusion), channel_id=1, source_target_pairs={{0,7},{1,6},{2,5},{3,4},{4,11},{5,10},{6,9},{7,8},{8,15},{9,14},{1... | collective-permute-start | bytes 786440 | tf_op jit(solution)/shard_map/ppermute | solution.py:109
  5.0 1.8 %collective-permute-start.2 = (bf16[128,1024]{1,0:T(8,128)(2,1)S(1)}, bf16[128,1024]{1,0:T(8,128)(2,1)S(1)}, u32[]{:S(2)}, u32[]{:S(2)}) collective-permute-start(bf16[128,1024]{1,0:T(8,128)(2,1)S(1)} %constant_dynamic-update-slice_fusion), channel_id=1, source_target_pairs={{0,6},{1,7},{2,4},{3,5},{4,10},{5,11},{6,8},{7,9},{8,14},{9,15},{1... | collective-permute-start | bytes 786440 | tf_op jit(solution)/shard_map/ppermute | solution.py:109
  6.8 0.1 collective-permute-start.1
  7.0 1.5 %collective-permute-start = (bf16[128,1024]{1,0:T(8,128)(2,1)S(1)}, bf16[128,1024]{1,0:T(8,128)(2,1)S(1)}, u32[]{:S(2)}, u32[]{:S(2)}) collective-permute-start(bf16[128,1024]{1,0:T(8,128)(2,1)S(1)} %constant_dynamic-update-slice_fusion), channel_id=1, source_target_pairs={{0,4},{1,5},{2,6},{3,7},{4,8},{5,9},{6,10},{7,11},{8,12},{9,13},{1... | collective-permute-start | bytes 786440 | tf_op jit(solution)/shard_map/ppermute | solution.py:109
  8.5 0.0 copy-done.5
  8.5 0.1 copy.10.refs_2_
  8.6 0.0 copy-done.6
  8.6 0.1 copy.11.refs_3_
  8.7 1.5 %shard_map.94 = (bf16[128,128]{1,0:T(8,128)(2,1)}, bf16[4,128,128]{2,1,0:T(8,128)(2,1)}) custom-call(s32[16]{0:T(128)} %doc_ref.1), custom_call_target="tpu_custom_call" | custom-call | tf_op jit(solution)/shard_map/pallas_call | solution.py:92
  10.2 2.1 %collective-permute-done.3.refs_9_ = bf16[128,1024]{1,0:T(8,128)(2,1)S(1)} collective-permute-done((bf16[128,1024]{1,0:T(8,128)(2,1)S(1)}, bf16[128,1024]{1,0:T(8,128)(2,1)S(1)}, u32[]{:S(2)}, u32[]{:S(2)}) %collective-permute-start.3) | collective-permute-done | bytes 262176 | tf_op jit(solution)/shard_map/ppermute | solution.py:109
  12.3 5.0 %collective-permute-done.2.refs_8_ = bf16[128,1024]{1,0:T(8,128)(2,1)S(1)} collective-permute-done((bf16[128,1024]{1,0:T(8,128)(2,1)S(1)}, bf16[128,1024]{1,0:T(8,128)(2,1)S(1)}, u32[]{:S(2)}, u32[]{:S(2)}) %collective-permute-start.2) | collective-permute-done | bytes 262176 | tf_op jit(solution)/shard_map/ppermute | solution.py:109
  17.3 2.0 %collective-permute-done.1.refs_7_ = bf16[128,1024]{1,0:T(8,128)(2,1)S(1)} collective-permute-done((bf16[128,1024]{1,0:T(8,128)(2,1)S(1)}, bf16[128,1024]{1,0:T(8,128)(2,1)S(1)}, u32[]{:S(2)}, u32[]{:S(2)}) %collective-permute-start.1) | collective-permute-done | bytes 262176 | tf_op jit(solution)/shard_map/ppermute | solution.py:109
  19.3 1.9 %collective-permute-done.refs_6_ = bf16[128,1024]{1,0:T(8,128)(2,1)S(1)} collective-permute-done((bf16[128,1024]{1,0:T(8,128)(2,1)S(1)}, bf16[128,1024]{1,0:T(8,128)(2,1)S(1)}, u32[]{:S(2)}, u32[]{:S(2)}) %collective-permute-start) | collective-permute-done | bytes 262176 | tf_op jit(solution)/shard_map/ppermute | solution.py:109
  21.2 0.0 copy-start
  21.2 1.2 %copy-done = bf16[128,4096]{1,0:T(8,128)(2,1)S(1)} copy-done((bf16[128,4096]{1,0:T(8,128)(2,1)S(1)}, bf16[128,4096]{1,0:T(8,128)(2,1)}, u32[]{:S(2)}) %copy-start) | copy-done | bytes 1048600
  22.4 0.0 copy-start.1
  22.4 1.2 %copy-done.1 = bf16[128,4096]{1,0:T(8,128)(2,1)S(1)} copy-done((bf16[128,4096]{1,0:T(8,128)(2,1)S(1)}, bf16[128,4096]{1,0:T(8,128)(2,1)}, u32[]{:S(2)}) %copy-start.1) | copy-done | bytes 1048600
  23.7 0.0 copy-start.2
  23.7 0.9 %copy-done.2 = bf16[4,128,128]{2,1,0:T(8,128)(2,1)S(1)} copy-done((bf16[4,128,128]{2,1,0:T(8,128)(2,1)S(1)}, bf16[4,128,128]{2,1,0:T(8,128)(2,1)}, u32[]{:S(2)}) %copy-start.2) | copy-done | bytes 131096
  24.6 0.0 copy-start.3
  24.6 0.8 %copy-done.3 = bf16[128,128]{1,0:T(8,128)(2,1)S(1)} copy-done((bf16[128,128]{1,0:T(8,128)(2,1)S(1)}, bf16[128,128]{1,0:T(8,128)(2,1)}, u32[]{:S(2)}) %copy-start.3) | copy-done | bytes 32792
  25.3 11.9 %shard_map.95 = (bf16[128,4096]{1,0:T(8,128)(2,1)}, f32[128,32]{1,0:T(8,128)S(1)}, f32[128,32]{1,0:T(8,128)S(1)}) custom-call(bf16[128,4096]{1,0:T(8,128)(2,1)S(1)} %copy-done, bf16[128,4096]{1,0:T(8,128)(2,1)S(1)} %copy-done.1, f32[128,32]{1,0:T(8,128)S(1)} %copy.10.refs_2_, f32[128,32]{1,0:T(8,128)S(1)} %copy.11.refs_3_, bf16[128,128]{1,0:T(8,128)(2,1)S(1)} %copy-done.3, ...), custom_call_target="tpu_custom_call" | custom-call | flops 1073741824 | bytes 4194304 | tf_op jit(solution)/shard_map/pallas_call | solution.py:111
  37.3 0.7 %copy.12 = f32[128,32]{0,1:T(8,128)} copy(f32[128,32]{1,0:T(8,128)S(1)} %get-tuple-element.8) | data formatting | bytes 32768 | tf_op jit(solution)/shard_map/pallas_call | solution.py:111
  37.9 0.7 %copy.13 = f32[128,32]{0,1:T(8,128)} copy(f32[128,32]{1,0:T(8,128)S(1)} %get-tuple-element.9) | data formatting | bytes 32768 | tf_op jit(solution)/shard_map/pallas_call | solution.py:111
  (1 shorter events, 0.0 us)
Async XLA Ops:
  0.6 1.0 %copy-start.4 = (bf16[128,512]{1,0:T(8,128)(2,1)S(1)}, bf16[128,512]{1,0:T(8,128)(2,1)}, u32[]{:S(2)}) copy-start(bf16[128,512]{1,0:T(8,128)(2,1)} %param.9) | copy-start | bytes 393220
  1.6 6.9 %copy-start.5 = (f32[128,32]{0,1:T(8,128)S(1)}, f32[128,32]{0,1:T(8,128)}, u32[]{:S(2)}) copy-start(f32[128,32]{0,1:T(8,128)} %param.11) | copy-start | bytes 49156
  1.6 7.0 %copy-start.6 = (f32[128,32]{0,1:T(8,128)S(1)}, f32[128,32]{0,1:T(8,128)}, u32[]{:S(2)}) copy-start(f32[128,32]{0,1:T(8,128)} %param.12) | copy-start | bytes 49156
  1.6 10.7 %collective-permute-start.3 = (bf16[128,1024]{1,0:T(8,128)(2,1)S(1)}, bf16[128,1024]{1,0:T(8,128)(2,1)S(1)}, u32[]{:S(2)}, u32[]{:S(2)}) collective-permute-start(bf16[128,1024]{1,0:T(8,128)(2,1)S(1)} %constant_dynamic-update-slice_fusion), channel_id=1, source_target_pairs={{0,7},{1,6},{2,5},{3,4},{4,11},{5,10},{6,9},{7,8},{8,15},{9,14},{1... | collective-permute-start | bytes 786440 | tf_op jit(solution)/shard_map/ppermute | solution.py:109
  5.0 12.3 %collective-permute-start.2 = (bf16[128,1024]{1,0:T(8,128)(2,1)S(1)}, bf16[128,1024]{1,0:T(8,128)(2,1)S(1)}, u32[]{:S(2)}, u32[]{:S(2)}) collective-permute-start(bf16[128,1024]{1,0:T(8,128)(2,1)S(1)} %constant_dynamic-update-slice_fusion), channel_id=1, source_target_pairs={{0,6},{1,7},{2,4},{3,5},{4,10},{5,11},{6,8},{7,9},{8,14},{9,15},{1... | collective-permute-start | bytes 786440 | tf_op jit(solution)/shard_map/ppermute | solution.py:109
  6.8 12.5 %collective-permute-start.1 = (bf16[128,1024]{1,0:T(8,128)(2,1)S(1)}, bf16[128,1024]{1,0:T(8,128)(2,1)S(1)}, u32[]{:S(2)}, u32[]{:S(2)}) collective-permute-start(bf16[128,1024]{1,0:T(8,128)(2,1)S(1)} %constant_dynamic-update-slice_fusion), channel_id=1, source_target_pairs={{0,5},{1,4},{2,7},{3,6},{4,9},{5,8},{6,11},{7,10},{8,13},{9,12},{1... | collective-permute-start | bytes 786440 | tf_op jit(solution)/shard_map/ppermute | solution.py:109
  7.0 14.2 %collective-permute-start = (bf16[128,1024]{1,0:T(8,128)(2,1)S(1)}, bf16[128,1024]{1,0:T(8,128)(2,1)S(1)}, u32[]{:S(2)}, u32[]{:S(2)}) collective-permute-start(bf16[128,1024]{1,0:T(8,128)(2,1)S(1)} %constant_dynamic-update-slice_fusion), channel_id=1, source_target_pairs={{0,4},{1,5},{2,6},{3,7},{4,8},{5,9},{6,10},{7,11},{8,12},{9,13},{1... | collective-permute-start | bytes 786440 | tf_op jit(solution)/shard_map/ppermute | solution.py:109
  21.2 1.2 %copy-start = (bf16[128,4096]{1,0:T(8,128)(2,1)S(1)}, bf16[128,4096]{1,0:T(8,128)(2,1)}, u32[]{:S(2)}) copy-start(bf16[128,4096]{1,0:T(8,128)(2,1)} %refs_0_.1) | copy-start | bytes 3145732
  22.4 1.2 %copy-start.1 = (bf16[128,4096]{1,0:T(8,128)(2,1)S(1)}, bf16[128,4096]{1,0:T(8,128)(2,1)}, u32[]{:S(2)}) copy-start(bf16[128,4096]{1,0:T(8,128)(2,1)} %refs_1_.1) | copy-start | bytes 3145732
  23.7 0.9 %copy-start.2 = (bf16[4,128,128]{2,1,0:T(8,128)(2,1)S(1)}, bf16[4,128,128]{2,1,0:T(8,128)(2,1)}, u32[]{:S(2)}) copy-start(bf16[4,128,128]{2,1,0:T(8,128)(2,1)} %get-tuple-element.6.refs_5_) | copy-start | bytes 393220
  24.6 0.8 %copy-start.3 = (bf16[128,128]{1,0:T(8,128)(2,1)S(1)}, bf16[128,128]{1,0:T(8,128)(2,1)}, u32[]{:S(2)}) copy-start(bf16[128,128]{1,0:T(8,128)(2,1)} %get-tuple-element.5.refs_4_) | copy-start | bytes 98308

commit v2 on v1

v2 whole, which is shorter than its diff:
```python
import functools
import math

import jax
import jax.numpy as jnp
from jax import lax
from jax.experimental import pallas as pl
from jax.experimental.pallas import tpu as pltpu
from jax.sharding import PartitionSpec as P

HD = 128
LANES = 128
HIDE = -1e30
LOG2E = math.log2(math.e)
VMEM = pl.BlockSpec(memory_space=pltpu.VMEM)
SMEM = pl.BlockSpec(memory_space=pltpu.SMEM)
PAIR = 2
PLAN = (
    ("0k", None, 0),
    ("0v", None, 0),
    ("1k", None, 1),
    ("2v", None, 2),
    ("1v", "0v", 1),
    ("2k", "0k", 2),
    ("3k", "1k", 2),
    ("3v", "2v", 1),
)
EARLY = (0,)
MASK_FLOPS = 2 * 10**10


def source(at, step, n_inner):
    return at ^ step if n_inner & (n_inner - 1) == 0 else lax.rem(at + step, n_inner)


def mask_kernel(steps, docs, doc_ref, mine_ref, hide_ref):
    rows = mine_ref.shape[0]
    n_inner = len(steps)
    outer_at = lax.axis_index("outer")
    inner_at = lax.axis_index("inner")
    lane = lax.broadcasted_iota(jnp.int32, (8, LANES), 1)
    far = jnp.full((8, LANES), 2**30, jnp.int32)

    def one(d, state):
        first, starts, ends = state
        last = first + doc_ref[d]
        return last, jnp.where(lane == d, first, starts), jnp.where(lane == d, last, ends)

    unused, starts, ends = lax.fori_loop(0, docs, one, (jnp.int32(0), far, far))
    tok = lax.broadcasted_iota(jnp.int32, (rows, LANES), 0)
    qpos = tok + (outer_at * n_inner + inner_at) * rows
    mine_ref[...] = jnp.where((starts[:1] <= qpos) & (qpos < ends[:1]), 1.0, 0.0).astype(jnp.bfloat16)
    for place, step in enumerate(steps):
        kpos = tok + ((outer_at - 1) * n_inner + source(inner_at, step, n_inner)) * rows
        hide_ref[pl.ds(place * rows, rows), :] = jnp.where(kpos < starts[:1], HIDE, 0.0).astype(jnp.bfloat16)


def rows_of(ref, heads):
    return jnp.concatenate([ref[pl.ds(x, 1), :] for x in heads], axis=1)


def work_of(kv_heads, group):
    return [(h, [h * group + g + k for k in range(PAIR)]) for h in range(kv_heads) for g in range(0, group, PAIR)]


def weigh_kernel(n_inner, early, kv_heads, group, scale, *refs):
    q_ref, old_ref, max_ref, sum_ref, mine_ref, hide_ref = refs[:6]
    k_refs = refs[6 : 6 + n_inner]
    v_refs = refs[6 + n_inner : 6 + n_inner + early]
    w_ref, acc_ref, top_ref, total_ref, inverse_ref = refs[6 + n_inner + early :]
    rows = q_ref.shape[0]
    split = early * rows
    work = work_of(kv_heads, group)

    def old_of(heads):
        return jnp.concatenate([old_ref[:, pl.ds(x * HD, HD)].T for x in heads], axis=1).astype(jnp.float32)

    def finish(heads, top, total, numer):
        inverse = 1.0 / total
        for k, x in enumerate(heads):
            cut = slice(k * rows, (k + 1) * rows)
            top_ref[pl.ds(x, 1), :] = top[:, cut]
            total_ref[pl.ds(x, 1), :] = total[:, cut]
            inverse_ref[pl.ds(x, 1), :] = inverse[:, cut]
            acc_ref[pl.ds(x * HD, HD), :] = numer[:, cut]

    live = lax.axis_index("outer") > 0

    @pl.when(live)
    def _():
        mine = jnp.concatenate([mine_ref[...]] * PAIR, axis=0)
        keys, vals = {}, {}

        def score(h, heads):
            if h not in keys:
                cols = pl.ds(h * HD, HD)
                keys[h] = jnp.concatenate([jnp.concatenate([k[:, cols] for k in k_refs], axis=0), hide_ref[...]], axis=1)
                vals[h] = jnp.concatenate([v[:, cols].T for v in v_refs], axis=1) if early else None
            q = jnp.concatenate([jnp.concatenate([q_ref[:, pl.ds(x * HD, HD)] for x in heads], axis=0), mine], axis=1)
            return lax.dot_general(keys[h], q, (((1,), (1,)), ((), ())), preferred_element_type=jnp.float32)

        def soften(s, heads):
            old_max = rows_of(max_ref, heads)
            top = jnp.maximum(old_max, jnp.max(s, axis=0, keepdims=True) * scale)
            w = jnp.exp2(s * (scale * LOG2E) - top * LOG2E)
            kept = rows_of(sum_ref, heads) * jnp.exp2((old_max - top) * LOG2E)
            total = kept + jnp.sum(w, axis=0, keepdims=True)
            w = w.astype(jnp.bfloat16)
            if split < w.shape[0]:
                w_ref[:, pl.ds(heads[0] * rows, len(heads) * rows)] = w[split:]
            return kept, top, total, w[:split]

        def mix(h, heads, kept, top, total, w):
            numer = old_of(heads) * kept
            if early:
                numer += jnp.dot(vals[h], w, preferred_element_type=jnp.float32)
            finish(heads, top, total, numer)

        scores, soft = {}, {}
        for t in range(len(work) + 2):
            if t < len(work):
                scores[t] = score(*work[t])
            if 0 <= t - 1 < len(work):
                soft[t - 1] = soften(scores.pop(t - 1), work[t - 1][1])
            if 0 <= t - 2 < len(work):
                mix(*work[t - 2], *soft.pop(t - 2))

    @pl.when(jnp.logical_not(live))
    def _():
        for h, heads in work:
            total = rows_of(sum_ref, heads)
            finish(heads, rows_of(max_ref, heads), total, old_of(heads) * total)


def mix_kernel(late, kv_heads, group, w_ref, acc_ref, inverse_ref, *refs):
    v_refs = refs[:late]
    out_ref, stage, sems = refs[late:]
    rows = out_ref.shape[0]
    wide = group * HD
    work = work_of(kv_heads, group)

    def flush(h):
        span = pl.ds(h * wide, wide)
        return pltpu.make_async_copy(stage.at[:, span], out_ref.at[:, span], sems.at[h])

    def finish(heads, numer):
        result = (numer * rows_of(inverse_ref, heads)).astype(jnp.bfloat16)
        for k, x in enumerate(heads):
            stage[:, pl.ds(x * HD, HD)] = result[:, k * rows : (k + 1) * rows].T
        if (heads[-1] + 1) % group == 0:
            flush(heads[0] // group).start()

    def numer_of(heads):
        return jnp.concatenate([acc_ref[pl.ds(x * HD, HD), :] for x in heads], axis=1)

    live = lax.axis_index("outer") > 0

    @pl.when(live)
    def _():
        vals = {}

        def mixed(h, heads):
            if h not in vals:
                cols = pl.ds(h * HD, HD)
                vals[h] = jnp.concatenate([v[:, cols].T for v in v_refs], axis=1)
            w = w_ref[:, pl.ds(heads[0] * rows, len(heads) * rows)]
            return jnp.dot(vals[h], w, preferred_element_type=jnp.float32)

        held = {}
        for t in range(len(work) + 1):
            if t < len(work):
                held[t] = mixed(*work[t])
            if t >= 1:
                heads = work[t - 1][1]
                finish(heads, numer_of(heads) + held.pop(t - 1))

    @pl.when(jnp.logical_not(live))
    def _():
        for h, heads in work:
            finish(heads, numer_of(heads))

    for h in range(kv_heads):
        flush(h).wait()


def move(keys, values, n_outer, n_inner):
    def direct(value, step):
        pairs = [
            (o * n_inner + source(i, step, n_inner), (o + 1) % n_outer * n_inner + i)
            for o in range(n_outer)
            for i in range(n_inner)
        ]
        return lax.ppermute(value, ("outer", "inner"), pairs)

    def within(value, step):
        return lax.ppermute(value, "inner", [(i ^ step, i) for i in range(n_inner)])

    own = {"k": keys, "v": values}
    got = {}
    if n_inner == 4:
        for piece, taken, step in PLAN:
            got[piece] = direct(own[piece[-1]], step) if taken is None else within(got[taken], step)
    else:
        for step in range(n_inner):
            for kind in "kv":
                got[f"{step}{kind}"] = direct(own[kind], step)
    return got


def body(queries, keys, values, acc_out, acc_max, acc_sum, doc_lengths):
    rows, width = queries.shape
    heads = acc_max.shape[1]
    kv_heads = keys.shape[1] // HD
    group = heads // kv_heads
    n_outer = lax.axis_size("outer")
    n_inner = lax.axis_size("inner")
    early = EARLY if n_inner == 4 else tuple(range(n_inner // 2))
    steps = early + tuple(step for step in range(n_inner) if step not in early)
    got = move(keys, values, n_outer, n_inner)
    mine, hide = pl.pallas_call(
        functools.partial(mask_kernel, steps, doc_lengths.shape[0]),
        out_shape=(
            jax.ShapeDtypeStruct((rows, LANES), jnp.bfloat16),
            jax.ShapeDtypeStruct((n_inner * rows, LANES), jnp.bfloat16),
        ),
        in_specs=[SMEM],
        out_specs=(VMEM,) * 2,
        compiler_params=pltpu.CompilerParams(vmem_limit_bytes=2 * 2**20),
        cost_estimate=pl.CostEstimate(flops=MASK_FLOPS, bytes_accessed=2**18, transcendentals=0),
    )(doc_lengths)
    late = n_inner - len(early)
    stat = jax.ShapeDtypeStruct((heads, rows), jnp.float32)
    area = rows * rows * heads
    w, acc, top, total, inverse = pl.pallas_call(
        functools.partial(weigh_kernel, n_inner, len(early), kv_heads, group, 1.0 / math.sqrt(HD)),
        out_shape=(
            jax.ShapeDtypeStruct((late * rows, heads * rows), jnp.bfloat16),
            jax.ShapeDtypeStruct((width, rows), jnp.float32),
            stat,
            stat,
            stat,
        ),
        in_specs=[VMEM] * (6 + n_inner + len(early)),
        out_specs=(VMEM,) * 5,
        compiler_params=pltpu.CompilerParams(vmem_limit_bytes=16 * 2**20),
        cost_estimate=pl.CostEstimate(
            flops=2 * area * HD * (n_inner + len(early)), bytes_accessed=2**20, transcendentals=area * n_inner
        ),
    )(
        queries,
        acc_out,
        acc_max.T,
        acc_sum.T,
        mine,
        hide,
        *[got[f"{step}k"] for step in steps],
        *[got[f"{step}v"] for step in early],
    )
    out = pl.pallas_call(
        functools.partial(mix_kernel, late, kv_heads, group),
        out_shape=jax.ShapeDtypeStruct((rows, width), jnp.bfloat16),
        in_specs=[VMEM] * (3 + late),
        out_specs=pl.BlockSpec(memory_space=pl.ANY),
        scratch_shapes=[pltpu.VMEM((rows, width), jnp.bfloat16), pltpu.SemaphoreType.DMA((kv_heads,))],
        compiler_params=pltpu.CompilerParams(vmem_limit_bytes=16 * 2**20),
        cost_estimate=pl.CostEstimate(flops=2 * area * HD * late, bytes_accessed=2**20, transcendentals=0),
    )(w, acc, inverse, *[got[f"{step}v"] for step in steps[len(early) :]])
    return out, top.T, total.T


def solution(mesh):
    split = P(("outer", "inner"), None)
    return jax.shard_map(
        body,
        mesh=mesh,
        in_specs=(split,) * 6 + (P(),),
        out_specs=(split,) * 3,
        check_vma=False,
    )
```

time: 38.9 us -> 21.5 us (0.55)
  the two profiles are of different devices: /device:TPU:0 before, /device:TPU:8 now
where the time goes in v2:
time: 21.5 us; the launch traced here: 21.1 us
  starting transfers between devices  10.2 us (47%)
  Pallas kernels  6.04 us (28%)
  waiting for transfers between devices  3.41 us (16%)
  between operations  0.7 us (3%)
  local copies, waits for them, and re-layouts  0.67 us (3%)
    ppermute x4, starting transfers between devices, direct(): return lax.ppermute(value, ('outer', 'inner'), pairs)  5.32 us
    ppermute x4, starting transfers between devices, within(): return lax.ppermute(value, 'inner', [(i ^ step, i) for i in range(n_inner)])  4.92 us
    pallas_call x1, Pallas kernels, body(): pl.pallas_call(functools.partial(weigh_kernel, n_inner, len(early), kv_he...  3.73 us
    ppermute x4, waiting for transfers between devices, within(): return lax.ppermute(value, 'inner', [(i ^ step, i) for i in range(n_inner)])  2.17 us
    pallas_call x1, Pallas kernels, body(): pl.pallas_call(functools.partial(mix_kernel, late, kv_heads, group), out_...  1.62 us
    ppermute x4, waiting for transfers between devices, direct(): return lax.ppermute(value, ('outer', 'inner'), pairs)  1.24 us
    pallas_call x1, Pallas kernels, body(): pl.pallas_call(functools.partial(mask_kernel, steps, doc_lengths.shape[0]...  0.69 us
    unnamed x10, local copies, waits for them, and re-layouts  0.67 us
  transfers between devices with their start and end apart: 8, of which 3 were waited for; matrix products, arithmetic and copies ran while one was open for 0% of the time, Pallas kernels for 21%

profile of v2, /device:TPU:8, one launch (start us, length us, event | category | flops | bytes accessed | tf_op | source)
XLA Modules:
  0.0 21.1 jit_solution(16385078437170729808)
XLA Ops:
  0.6 0.0 copy-start.3
  0.6 0.0 copy-start.2
  0.7 0.0 copy-start.1
  0.7 0.0 copy-start
  0.7 1.0 %collective-permute-start.1 = (bf16[128,512]{1,0:T(8,128)(2,1)}, bf16[128,512]{1,0:T(8,128)(2,1)S(1)}, u32[]{:S(2)}, u32[]{:S(2)}) collective-permute-start(bf16[128,512]{1,0:T(8,128)(2,1)} %param.8), channel_id=1, source_target_pairs={{1,4},{0,5},{3,6},{2,7},{5,8},{4,9},{7,10},{6,11},{9,12},{8,13},{1... | collective-permute-start | bytes 393224 | tf_op jit(solution)/shard_map/ppermute | solution.py:193
  1.7 1.7 %collective-permute-start = (bf16[128,512]{1,0:T(8,128)(2,1)}, bf16[128,512]{1,0:T(8,128)(2,1)S(1)}, u32[]{:S(2)}, u32[]{:S(2)}) collective-permute-start(bf16[128,512]{1,0:T(8,128)(2,1)} %param.8), channel_id=1, source_target_pairs={{0,4},{1,5},{2,6},{3,7},{4,8},{5,9},{6,10},{7,11},{8,12},{9,13},{1... | collective-permute-start | bytes 393224 | tf_op jit(solution)/shard_map/ppermute | solution.py:193
  3.3 1.1 %collective-permute-start.6 = (bf16[128,512]{1,0:T(8,128)(2,1)}, bf16[128,512]{1,0:T(8,128)(2,1)S(1)}, u32[]{:S(2)}, u32[]{:S(2)}) collective-permute-start(bf16[128,512]{1,0:T(8,128)(2,1)} %param.9), channel_id=1, source_target_pairs={{2,4},{3,5},{0,6},{1,7},{6,8},{7,9},{4,10},{5,11},{10,12},{11,13},... | collective-permute-start | bytes 393224 | tf_op jit(solution)/shard_map/ppermute | solution.py:193
  4.5 1.5 %collective-permute-start.4 = (bf16[128,512]{1,0:T(8,128)(2,1)}, bf16[128,512]{1,0:T(8,128)(2,1)S(1)}, u32[]{:S(2)}, u32[]{:S(2)}) collective-permute-start(bf16[128,512]{1,0:T(8,128)(2,1)} %param.9), channel_id=1, source_target_pairs={{0,4},{1,5},{2,6},{3,7},{4,8},{5,9},{6,10},{7,11},{8,12},{9,13},{1... | collective-permute-start | bytes 393224 | tf_op jit(solution)/shard_map/ppermute | solution.py:193
  6.0 0.3 %collective-permute-done.1.refs_7_ = bf16[128,512]{1,0:T(8,128)(2,1)S(1)} collective-permute-done((bf16[128,512]{1,0:T(8,128)(2,1)}, bf16[128,512]{1,0:T(8,128)(2,1)S(1)}, u32[]{:S(2)}, u32[]{:S(2)}) %collective-permute-start.1) | collective-permute-done | bytes 131104 | tf_op jit(solution)/shard_map/ppermute | solution.py:193
  6.3 1.5 %collective-permute-start.3 = (bf16[128,512]{1,0:T(8,128)(2,1)S(1)}, bf16[128,512]{1,0:T(8,128)(2,1)S(1)}, u32[]{:S(2)}, u32[]{:S(2)}) collective-permute-start(bf16[128,512]{1,0:T(8,128)(2,1)S(1)} %collective-permute-done.1.refs_7_), channel_id=1, source_target_pairs={{2,0},{3,1},{0,2},{1,3},{6,4},{7,5},{4,6},{5,7},{10,8},{11,9},{8,1... | collective-permute-start | bytes 393224 | tf_op jit(solution)/shard_map/ppermute | solution.py:196
  7.9 0.0 collective-permute-done.refs_6_
  7.9 1.4 %collective-permute-start.2 = (bf16[128,512]{1,0:T(8,128)(2,1)S(1)}, bf16[128,512]{1,0:T(8,128)(2,1)S(1)}, u32[]{:S(2)}, u32[]{:S(2)}) collective-permute-start(bf16[128,512]{1,0:T(8,128)(2,1)S(1)} %collective-permute-done.refs_6_), channel_id=1, source_target_pairs={{2,0},{3,1},{0,2},{1,3},{6,4},{7,5},{4,6},{5,7},{10,8},{11,9},{8,1... | collective-permute-start | bytes 393224 | tf_op jit(solution)/shard_map/ppermute | solution.py:196
  9.2 0.9 %collective-permute-done.6.refs_1_ = bf16[128,512]{1,0:T(8,128)(2,1)S(1)} collective-permute-done((bf16[128,512]{1,0:T(8,128)(2,1)}, bf16[128,512]{1,0:T(8,128)(2,1)S(1)}, u32[]{:S(2)}, u32[]{:S(2)}) %collective-permute-start.6) | collective-permute-done | bytes 131104 | tf_op jit(solution)/shard_map/ppermute | solution.py:193
  10.1 0.5 %collective-permute-start.7 = (bf16[128,512]{1,0:T(8,128)(2,1)S(1)}, bf16[128,512]{1,0:T(8,128)(2,1)S(1)}, u32[]{:S(2)}, u32[]{:S(2)}) collective-permute-start(bf16[128,512]{1,0:T(8,128)(2,1)S(1)} %collective-permute-done.6.refs_1_), channel_id=1, source_target_pairs={{1,0},{0,1},{3,2},{2,3},{5,4},{4,5},{7,6},{6,7},{9,8},{8,9},{11,10... | collective-permute-start | bytes 393224 | tf_op jit(solution)/shard_map/ppermute | solution.py:196
  10.6 0.0 collective-permute-done.4.refs_10_
  10.6 1.6 %collective-permute-start.5 = (bf16[128,512]{1,0:T(8,128)(2,1)S(1)}, bf16[128,512]{1,0:T(8,128)(2,1)S(1)}, u32[]{:S(2)}, u32[]{:S(2)}) collective-permute-start(bf16[128,512]{1,0:T(8,128)(2,1)S(1)} %collective-permute-done.4.refs_10_), channel_id=1, source_target_pairs={{1,0},{0,1},{3,2},{2,3},{5,4},{4,5},{7,6},{6,7},{9,8},{8,9},{11,10... | collective-permute-start | bytes 393224 | tf_op jit(solution)/shard_map/ppermute | solution.py:196
  12.2 0.0 copy-start.4
  12.2 0.7 %copy-done.4 = s32[16]{0:T(128)S(1)} copy-done((s32[16]{0:T(128)S(1)}, s32[16]{0:T(128)}, u32[]{:S(2)}) %copy-start.4) | copy-done | bytes 88
  12.8 0.7 %shard_map.94 = (bf16[128,128]{1,0:T(8,128)(2,1)S(1)}, bf16[512,128]{1,0:T(8,128)(2,1)S(1)}) custom-call(s32[16]{0:T(128)S(1)} %copy-done.4), custom_call_target="tpu_custom_call" | custom-call | flops 20000000000 | bytes 262144 | tf_op jit(solution)/shard_map/pallas_call | solution.py:220
  13.5 0.0 collective-permute-done.3.refs_9_
  13.5 2.2 %collective-permute-done.2.refs_8_ = bf16[128,512]{1,0:T(8,128)(2,1)S(1)} collective-permute-done((bf16[128,512]{1,0:T(8,128)(2,1)S(1)}, bf16[128,512]{1,0:T(8,128)(2,1)S(1)}, u32[]{:S(2)}, u32[]{:S(2)}) %collective-permute-start.2) | collective-permute-done | bytes 131104 | tf_op jit(solution)/shard_map/ppermute | solution.py:196
  15.7 0.0 copy-done.3
  15.7 0.0 copy-done.2
  15.7 0.0 copy-done.1
  15.7 0.0 copy-done
  15.7 3.7 %shard_map.95 = (bf16[384,4096]{1,0:T(8,128)(2,1)S(1)}, f32[4096,128]{1,0:T(8,128)S(1)}, f32[32,128]{1,0:T(8,128)}, f32[32,128]{1,0:T(8,128)}, f32[32,128]{1,0:T(8,128)S(1)}) custom-call(bf16[128,4096]{1,0:T(8,128)(2,1)S(1)} %copy-done, bf16[128,4096]{1,0:T(8,128)(2,1)S(1)} %copy-done.1, f32[32,128]{1,0:T(8,128)S(1)} %bitcast.4, f32[32,128]{1,0:T(8,128)S(1)} %bitcast.5, ...), custom_call_target="tpu_custom_call" | custom-call | flops 671088640 | bytes 1048576 | tf_op jit(solution)/shard_map/pallas_call | solution.py:234
  19.4 0.0 collective-permute-done.7.refs_2_
  19.4 0.0 collective-permute-done.5.refs_0_
  19.4 1.6 %shard_map.96 = bf16[128,4096]{1,0:T(8,128)(2,1)} custom-call(bf16[384,4096]{1,0:T(8,128)(2,1)S(1)} %get-tuple-element.12.w_ref, f32[4096,128]{1,0:T(8,128)S(1)} %get-tuple-element.13.acc_ref, f32[32,128]{1,0:T(8,128)S(1)} %get-tuple-element.14.inverse_ref, bf16[128,512]{1,0:T(8,128)(2,1)S(1)} %collective-permute-done.5.refs_0_, ...), custom_call_target="tpu_custom_call" | custom-call | flops 402653184 | bytes 1048576 | tf_op jit(solution)/shard_map/pallas_call | solution.py:259
Async XLA Ops:
  0.6 15.1 %copy-start.3 = (f32[128,32]{0,1:T(8,128)S(1)}, f32[128,32]{0,1:T(8,128)}, u32[]{:S(2)}) copy-start(f32[128,32]{0,1:T(8,128)} %param.12) | copy-start | bytes 49156
  0.6 15.0 %copy-start.2 = (f32[128,32]{0,1:T(8,128)S(1)}, f32[128,32]{0,1:T(8,128)}, u32[]{:S(2)}) copy-start(f32[128,32]{0,1:T(8,128)} %param.11) | copy-start | bytes 49156
  0.7 15.0 %copy-start.1 = (bf16[128,4096]{1,0:T(8,128)(2,1)S(1)}, bf16[128,4096]{1,0:T(8,128)(2,1)}, u32[]{:S(2)}) copy-start(bf16[128,4096]{1,0:T(8,128)(2,1)} %refs_1_.1) | copy-start | bytes 3145732
  0.7 15.0 %copy-start = (bf16[128,4096]{1,0:T(8,128)(2,1)S(1)}, bf16[128,4096]{1,0:T(8,128)(2,1)}, u32[]{:S(2)}) copy-start(bf16[128,4096]{1,0:T(8,128)(2,1)} %refs_0_.1) | copy-start | bytes 3145732
  0.7 5.7 %collective-permute-start.1 = (bf16[128,512]{1,0:T(8,128)(2,1)}, bf16[128,512]{1,0:T(8,128)(2,1)S(1)}, u32[]{:S(2)}, u32[]{:S(2)}) collective-permute-start(bf16[128,512]{1,0:T(8,128)(2,1)} %param.8), channel_id=1, source_target_pairs={{1,4},{0,5},{3,6},{2,7},{5,8},{4,9},{7,10},{6,11},{9,12},{8,13},{1... | collective-permute-start | bytes 393224 | tf_op jit(solution)/shard_map/ppermute | solution.py:193
  1.7 6.2 %collective-permute-start = (bf16[128,512]{1,0:T(8,128)(2,1)}, bf16[128,512]{1,0:T(8,128)(2,1)S(1)}, u32[]{:S(2)}, u32[]{:S(2)}) collective-permute-start(bf16[128,512]{1,0:T(8,128)(2,1)} %param.8), channel_id=1, source_target_pairs={{0,4},{1,5},{2,6},{3,7},{4,8},{5,9},{6,10},{7,11},{8,12},{9,13},{1... | collective-permute-start | bytes 393224 | tf_op jit(solution)/shard_map/ppermute | solution.py:193
  3.3 6.8 %collective-permute-start.6 = (bf16[128,512]{1,0:T(8,128)(2,1)}, bf16[128,512]{1,0:T(8,128)(2,1)S(1)}, u32[]{:S(2)}, u32[]{:S(2)}) collective-permute-start(bf16[128,512]{1,0:T(8,128)(2,1)} %param.9), channel_id=1, source_target_pairs={{2,4},{3,5},{0,6},{1,7},{6,8},{7,9},{4,10},{5,11},{10,12},{11,13},... | collective-permute-start | bytes 393224 | tf_op jit(solution)/shard_map/ppermute | solution.py:193
  4.5 6.1 %collective-permute-start.4 = (bf16[128,512]{1,0:T(8,128)(2,1)}, bf16[128,512]{1,0:T(8,128)(2,1)S(1)}, u32[]{:S(2)}, u32[]{:S(2)}) collective-permute-start(bf16[128,512]{1,0:T(8,128)(2,1)} %param.9), channel_id=1, source_target_pairs={{0,4},{1,5},{2,6},{3,7},{4,8},{5,9},{6,10},{7,11},{8,12},{9,13},{1... | collective-permute-start | bytes 393224 | tf_op jit(solution)/shard_map/ppermute | solution.py:193
  6.3 7.2 %collective-permute-start.3 = (bf16[128,512]{1,0:T(8,128)(2,1)S(1)}, bf16[128,512]{1,0:T(8,128)(2,1)S(1)}, u32[]{:S(2)}, u32[]{:S(2)}) collective-permute-start(bf16[128,512]{1,0:T(8,128)(2,1)S(1)} %collective-permute-done.1.refs_7_), channel_id=1, source_target_pairs={{2,0},{3,1},{0,2},{1,3},{6,4},{7,5},{4,6},{5,7},{10,8},{11,9},{8,1... | collective-permute-start | bytes 393224 | tf_op jit(solution)/shard_map/ppermute | solution.py:196
  7.9 7.8 %collective-permute-start.2 = (bf16[128,512]{1,0:T(8,128)(2,1)S(1)}, bf16[128,512]{1,0:T(8,128)(2,1)S(1)}, u32[]{:S(2)}, u32[]{:S(2)}) collective-permute-start(bf16[128,512]{1,0:T(8,128)(2,1)S(1)} %collective-permute-done.refs_6_), channel_id=1, source_target_pairs={{2,0},{3,1},{0,2},{1,3},{6,4},{7,5},{4,6},{5,7},{10,8},{11,9},{8,1... | collective-permute-start | bytes 393224 | tf_op jit(solution)/shard_map/ppermute | solution.py:196
  10.1 9.3 %collective-permute-start.7 = (bf16[128,512]{1,0:T(8,128)(2,1)S(1)}, bf16[128,512]{1,0:T(8,128)(2,1)S(1)}, u32[]{:S(2)}, u32[]{:S(2)}) collective-permute-start(bf16[128,512]{1,0:T(8,128)(2,1)S(1)} %collective-permute-done.6.refs_1_), channel_id=1, source_target_pairs={{1,0},{0,1},{3,2},{2,3},{5,4},{4,5},{7,6},{6,7},{9,8},{8,9},{11,10... | collective-permute-start | bytes 393224 | tf_op jit(solution)/shard_map/ppermute | solution.py:196
  10.6 8.8 %collective-permute-start.5 = (bf16[128,512]{1,0:T(8,128)(2,1)S(1)}, bf16[128,512]{1,0:T(8,128)(2,1)S(1)}, u32[]{:S(2)}, u32[]{:S(2)}) collective-permute-start(bf16[128,512]{1,0:T(8,128)(2,1)S(1)} %collective-permute-done.4.refs_10_), channel_id=1, source_target_pairs={{1,0},{0,1},{3,2},{2,3},{5,4},{4,5},{7,6},{6,7},{9,8},{8,9},{11,10... | collective-permute-start | bytes 393224 | tf_op jit(solution)/shard_map/ppermute | solution.py:196
  12.2 0.7 %copy-start.4 = (s32[16]{0:T(128)S(1)}, s32[16]{0:T(128)}, u32[]{:S(2)}) copy-start(s32[16]{0:T(128)} %doc_ref.1) | copy-start | bytes 196

commit v3 on v2

v3 whole, which is shorter than its diff:
```python
import functools
import math

import jax
import jax.numpy as jnp
from jax import lax
from jax.experimental import pallas as pl
from jax.experimental.pallas import tpu as pltpu
from jax.sharding import PartitionSpec as P

HD = 128
LANES = 128
HIDE = -1e30
LOG2E = math.log2(math.e)
VMEM = pl.BlockSpec(memory_space=pltpu.VMEM)
SMEM = pl.BlockSpec(memory_space=pltpu.SMEM)
PAIR = 1
MIX_PAIR = 2
FLUSH = 8
PLAN = (
    (("0k",), (), 0),
    (("1k",), (), 1),
    (("2k",), (), 2),
    (("0v",), (), 0),
    (("2v",), (), 2),
    (("3k",), ("1k",), 2),
    (("1v", "3v"), ("0v", "2v"), 1),
)
STAGES = ((0, 1), (2,), (3,))
EARLY = ()
TIES = {}
AHEAD_FLOPS = 2 * 10**10


def source(at, step, n_inner):
    return at ^ step if n_inner & (n_inner - 1) == 0 else lax.rem(at + step, n_inner)


def ahead_kernel(out_ref):
    out_ref[...] = jnp.zeros_like(out_ref)


def masks(steps, n_inner, doc_ref, mine_ref, hide_refs):
    rows = mine_ref.shape[0]
    outer_at = lax.axis_index("outer")
    inner_at = lax.axis_index("inner")
    lane = lax.broadcasted_iota(jnp.int32, (8, LANES), 1)
    far = jnp.full((8, LANES), 2**30, jnp.int32)

    def one(d, state):
        first, starts, ends = state
        last = first + doc_ref[d]
        return last, jnp.where(lane == d, first, starts), jnp.where(lane == d, last, ends)

    unused, starts, ends = lax.fori_loop(0, doc_ref.shape[0], one, (jnp.int32(0), far, far), unroll=4)
    tok = lax.broadcasted_iota(jnp.int32, (rows, LANES), 0)
    qpos = tok + (outer_at * n_inner + inner_at) * rows
    mine_ref[...] = jnp.where((starts[:1] <= qpos) & (qpos < ends[:1]), 1.0, 0.0).astype(jnp.bfloat16)
    for hide_ref, held in zip(hide_refs, steps):
        for place, step in enumerate(held):
            kpos = tok + ((outer_at - 1) * n_inner + source(inner_at, step, n_inner)) * rows
            hide_ref[pl.ds(place * rows, rows), :] = jnp.where(kpos < starts[:1], HIDE, 0.0).astype(jnp.bfloat16)


def rows_of(ref, heads):
    return jnp.concatenate([ref[pl.ds(x, 1), :] for x in heads], axis=1)


def work_of(kv_heads, group, pair):
    return [(h, [h * group + g + k for k in range(pair)]) for h in range(kv_heads) for g in range(0, group, pair)]


def weigh_kernel(stages, at, n_inner, early, k_at, v_at, kv_heads, group, scale, *refs):
    begin, end = at == 0, at + 1 == len(stages)
    refs = list(refs)
    if begin:
        doc_ref, unused, old_ref = refs[:3]
        mine_ref, hide_ref = refs[-2:]
        refs = refs[3:-2]
    else:
        mine_ref, hide_ref = refs[:2]
        refs = refs[2:]
    q_ref, max_ref, sum_ref = refs[:3]
    rows = q_ref.shape[0]
    k_refs = [refs[3 + which].at[pl.ds(first, rows)] for which, first in k_at]
    v_refs = [refs[3 + which].at[pl.ds(first, rows)] for which, first in v_at]
    refs = refs[3 + 1 + max(which for which, first in k_at + v_at) :]
    w_ref, top_ref, total_ref = refs[:3]
    refs = refs[3:]
    if end:
        inverse_ref = refs.pop(0)
    if not begin:
        shrink_ref = refs.pop(0)
    if begin:
        acc_ref = refs.pop(0)
        if len(stages) > 1:
            later_mine_ref, later_refs = refs[0], refs[1:]
    split = early * rows
    work = work_of(kv_heads, group, PAIR)
    live = lax.axis_index("outer") > 0

    def finish(heads, top, total, shrink, numer):
        inverse = 1.0 / total if end else None
        for k, x in enumerate(heads):
            cut = slice(k * rows, (k + 1) * rows)
            top_ref[pl.ds(x, 1), :] = top[:, cut]
            total_ref[pl.ds(x, 1), :] = total[:, cut]
            if end:
                inverse_ref[pl.ds(x, 1), :] = inverse[:, cut]
            if begin:
                acc_ref[pl.ds(x * HD, HD), :] = numer[:, cut]
            else:
                shrink_ref[pl.ds(x, 1), :] = shrink[:, cut]

    def old_of(heads):
        return jnp.concatenate([old_ref[:, pl.ds(x * HD, HD)].T for x in heads], axis=1).astype(jnp.float32)

    @pl.when(live)
    def _():
        if begin:
            masks(stages, n_inner, doc_ref, mine_ref, [hide_ref] + list(later_refs if len(stages) > 1 else []))
            if len(stages) > 1:
                later_mine_ref[...] = mine_ref[...]
        mine = jnp.concatenate([mine_ref[...]] * PAIR, axis=0)
        keys, vals = {}, {}

        def score(h, heads):
            if h not in keys:
                cols = pl.ds(h * HD, HD)
                keys[h] = jnp.concatenate([jnp.concatenate([k[:, cols] for k in k_refs], axis=0), hide_ref[...]], axis=1)
                vals[h] = jnp.concatenate([v[:, cols].T for v in v_refs], axis=1) if early else None
            q = jnp.concatenate([jnp.concatenate([q_ref[:, pl.ds(x * HD, HD)] for x in heads], axis=0), mine], axis=1)
            return lax.dot_general(keys[h], q, (((1,), (1,)), ((), ())), preferred_element_type=jnp.float32)

        def soften(s, heads):
            old_max = rows_of(max_ref, heads)
            top = jnp.maximum(old_max, jnp.max(s, axis=0, keepdims=True) * scale)
            w = jnp.exp2(s * (scale * LOG2E) - top * LOG2E)
            shrink = jnp.exp2((old_max - top) * LOG2E)
            kept = rows_of(sum_ref, heads) * shrink
            total = kept + jnp.sum(w, axis=0, keepdims=True)
            w = w.astype(jnp.bfloat16)
            if split < w.shape[0]:
                w_ref[:, pl.ds(heads[0] * rows, len(heads) * rows)] = w[split:]
            return kept, top, total, shrink, w[:split]

        def mix(h, heads, kept, top, total, shrink, w):
            numer = old_of(heads) * kept if begin else None
            if early:
                numer += jnp.dot(vals[h], w, preferred_element_type=jnp.float32)
            finish(heads, top, total, shrink, numer)

        scores, soft = {}, {}
        for t in range(len(work) + 2):
            if t < len(work):
                scores[t] = score(*work[t])
            if 0 <= t - 1 < len(work):
                soft[t - 1] = soften(scores.pop(t - 1), work[t - 1][1])
            if 0 <= t - 2 < len(work):
                mix(*work[t - 2], *soft.pop(t - 2))

    @pl.when(jnp.logical_not(live))
    def _():
        for h, heads in work:
            total = rows_of(sum_ref, heads)
            numer = old_of(heads) * total if begin else None
            finish(heads, rows_of(max_ref, heads), total, jnp.ones_like(total), numer)


def mix_kernel(stages, v_at, kv_heads, group, *refs):
    out_ref, top_out, total_out, stage, sems, stat_sems = refs[-6:]
    top_ref, total_ref = refs[:2]
    refs = refs[2:]
    rows = out_ref.shape[0]
    count = len(v_at)
    stats = [
        pltpu.make_async_copy(top_ref, top_out, stat_sems.at[0]),
        pltpu.make_async_copy(total_ref, total_out, stat_sems.at[1]),
    ]
    for copy in stats:
        copy.start()
    w_refs, shrink_refs = refs[:count], refs[count : 2 * count - 1]
    acc_ref, inverse_ref = refs[2 * count - 1 : 2 * count + 1]
    refs = refs[2 * count + 1 :]
    v_refs = [[refs[which].at[pl.ds(first, rows)] for which, first in held] for held in v_at]
    wide = FLUSH * HD
    work = work_of(kv_heads, group, MIX_PAIR)

    def flush(h):
        span = pl.ds(h * wide, wide)
        return pltpu.make_async_copy(stage.at[:, span], out_ref.at[:, span], sems.at[h])

    def finish(heads, numer):
        result = (numer * rows_of(inverse_ref, heads)).astype(jnp.bfloat16)
        for k, x in enumerate(heads):
            stage[:, pl.ds(x * HD, HD)] = result[:, k * rows : (k + 1) * rows].T
        if (heads[-1] + 1) % FLUSH == 0:
            flush(heads[-1] // FLUSH).start()

    def numer_of(heads):
        return jnp.concatenate([acc_ref[pl.ds(x * HD, HD), :] for x in heads], axis=1)

    live = lax.axis_index("outer") > 0

    @pl.when(live)
    def _():
        vals = {}

        def mixed(h, heads):
            if h not in vals:
                cols = pl.ds(h * HD, HD)
                vals[h] = [jnp.concatenate([v[:, cols].T for v in held], axis=1) if held else None for held in v_refs]
            at = pl.ds(heads[0] * rows, len(heads) * rows)
            return [
                jnp.dot(v, w[:, at], preferred_element_type=jnp.float32) if v is not None else None
                for v, w in zip(vals[h], w_refs)
            ]

        def close(heads, parts):
            numer = numer_of(heads)
            for at, part in enumerate(parts):
                if part is not None:
                    numer = numer + part
                if at + 1 < len(parts):
                    numer = numer * rows_of(shrink_refs[at], heads)
            finish(heads, numer)

        held = {}
        for t in range(len(work) + 1):
            if t < len(work):
                held[t] = mixed(*work[t])
            if t >= 1:
                close(work[t - 1][1], held.pop(t - 1))

    @pl.when(jnp.logical_not(live))
    def _():
        for h, heads in work:
            finish(heads, numer_of(heads))

    for h in range(kv_heads * group // FLUSH):
        flush(h).wait()
    for copy in stats:
        copy.wait()


def move(keys, values, n_outer, n_inner):
    def direct(value, step):
        pairs = [
            (o * n_inner + (source(i, step, n_inner) if o + 1 < n_outer else i), (o + 1) % n_outer * n_inner + i)
            for o in range(n_outer)
            for i in range(n_inner)
        ]
        return lax.ppermute(value, ("outer", "inner"), pairs)

    def within(value, step):
        return lax.ppermute(value, "inner", [(i ^ step, i) for i in range(n_inner)])

    own = {"k": keys, "v": values}
    rows = keys.shape[0]
    got = {}
    if n_inner == 4:
        plan = PLAN
    else:
        plan = [((f"{step}{kind}",), (), step) for kind in "kv" for step in range(n_inner)]
    for pieces, taken, step in plan:
        after = [x for x in TIES.get(pieces[0], ()) if n_inner == 4]
        if taken:
            parts = [got[x][0][got[x][1] : got[x][1] + rows] if got[x][0].shape[0] > rows else got[x][0] for x in taken]
            sent = jnp.concatenate(parts, axis=0) if len(parts) > 1 else parts[0]
        else:
            sent = own[pieces[0][-1]]
        if after:
            held = lax.optimization_barrier((sent, *[got[x][0] for x in after]))
            sent = held[0]
            for x, array in zip(after, held[1:]):
                got[x] = (array, got[x][1])
        moved = within(sent, step) if taken else direct(sent, step)
        for place, piece in enumerate(pieces):
            got[piece] = (moved, place * rows)
    return got


def gather(got, pieces):
    arrays, at = [], []
    for piece in pieces:
        array, first = got[piece]
        which = next((n for n, known in enumerate(arrays) if known is array), len(arrays))
        if which == len(arrays):
            arrays.append(array)
        at.append((which, first))
    return arrays, at


def body(queries, keys, values, acc_out, acc_max, acc_sum, doc_lengths):
    rows, width = queries.shape
    heads = acc_max.shape[1]
    kv_heads = keys.shape[1] // HD
    group = heads // kv_heads
    n_outer = lax.axis_size("outer")
    n_inner = lax.axis_size("inner")
    if n_inner == 4:
        stages, early = STAGES, EARLY
    else:
        half = n_inner // 2
        stages, early = (tuple(range(half)), tuple(range(half, n_inner))), ()
    got = move(keys, values, n_outer, n_inner)
    ahead = pl.pallas_call(
        ahead_kernel,
        out_shape=jax.ShapeDtypeStruct((8, LANES), jnp.float32),
        out_specs=VMEM,
        compiler_params=pltpu.CompilerParams(vmem_limit_bytes=2**20),
        cost_estimate=pl.CostEstimate(flops=AHEAD_FLOPS, bytes_accessed=4096, transcendentals=0),
    )()
    stat = jax.ShapeDtypeStruct((heads, rows), jnp.float32)
    area = rows * rows * heads
    tile = jax.ShapeDtypeStruct((rows, LANES), jnp.bfloat16)

    def hide_of(steps):
        return jax.ShapeDtypeStruct((len(steps) * rows, LANES), jnp.bfloat16)

    ws, shrinks, late = [], [], []
    top, total = acc_max.T, acc_sum.T
    for at, steps in enumerate(stages):
        begin, end = at == 0, at + 1 == len(stages)
        now = early if begin else ()
        late.append([step for step in steps if step not in now])
        arrays, places = gather(got, [f"{step}k" for step in steps] + [f"{step}v" for step in now])
        operands = [doc_lengths, ahead, acc_out] if begin else [mine, hides[at - 1]]
        operands += [queries, top, total, *arrays]
        out_shape = [jax.ShapeDtypeStruct((max(1, len(late[-1])) * rows, heads * rows), jnp.bfloat16), stat, stat]
        out_shape += [stat] * ((not begin) + end)
        if begin:
            out_shape.append(jax.ShapeDtypeStruct((width, rows), jnp.float32))
            out_shape += [tile] + [hide_of(steps) for steps in stages[1:]] if not end else []
        outs = pl.pallas_call(
            functools.partial(
                weigh_kernel,
                stages,
                at,
                n_inner,
                len(now),
                places[: len(steps)],
                places[len(steps) :],
                kv_heads,
                group,
                1.0 / math.sqrt(HD),
            ),
            out_shape=tuple(out_shape),
            in_specs=([SMEM] if begin else [VMEM]) + [VMEM] * (len(operands) - 1),
            out_specs=(VMEM,) * len(out_shape),
            scratch_shapes=[pltpu.VMEM(x.shape, x.dtype) for x in (tile, hide_of(steps))] if begin else [],
            compiler_params=pltpu.CompilerParams(vmem_limit_bytes=12 * 2**20),
            cost_estimate=pl.CostEstimate(
                flops=2 * area * HD * (len(steps) + len(now)), bytes_accessed=2**20, transcendentals=area * len(steps)
            ),
        )(*operands)
        outs = list(outs)
        ws.append(outs[0])
        top, total = outs[1:3]
        outs = outs[3:]
        if end:
            inverse = outs.pop(0)
        if not begin:
            shrinks.append(outs.pop(0))
        else:
            acc = outs.pop(0)
            mine, hides = (outs[0], outs[1:]) if not end else (None, None)
    arrays, places = gather(got, [f"{step}v" for held in late for step in held])
    places = iter(places)
    v_at = [[next(places) for step in held] for held in late]
    out, top, total = pl.pallas_call(
        functools.partial(mix_kernel, stages, v_at, kv_heads, group),
        out_shape=(jax.ShapeDtypeStruct((rows, width), jnp.bfloat16), stat, stat),
        in_specs=[VMEM] * (2 * len(stages) + 3 + len(arrays)),
        out_specs=(pl.BlockSpec(memory_space=pl.ANY),) * 3,
        scratch_shapes=[
            pltpu.VMEM((rows, width), jnp.bfloat16),
            pltpu.SemaphoreType.DMA((heads // FLUSH,)),
            pltpu.SemaphoreType.DMA((2,)),
        ],
        compiler_params=pltpu.CompilerParams(vmem_limit_bytes=12 * 2**20),
        cost_estimate=pl.CostEstimate(flops=2 * area * HD * n_inner, bytes_accessed=2**20, transcendentals=0),
    )(top, total, *ws, *shrinks, acc, inverse, *arrays)
    return out, top.T, total.T


def solution(mesh):
    split = P(("outer", "inner"), None)
    return jax.shard_map(
        body,
        mesh=mesh,
        in_specs=(split,) * 6 + (P(),),
        out_specs=(split,) * 3,
        check_vma=False,
    )
```

time: 21.5 us -> 18.7 us (0.87)
  the two profiles are of different devices: /device:TPU:8 before, /device:TPU:0 now
where the time goes in v3:
time: 18.7 us; the launch traced here: 18.5 us
  starting transfers between devices  10.7 us (57%)
  waiting for transfers between devices  4.98 us (27%)
  Pallas kernels  2.09 us (11%)
  between operations  0.74 us (4%)
    ppermute x5, starting transfers between devices, direct(): return lax.ppermute(value, ('outer', 'inner'), pairs)  7.17 us
    ppermute x2, starting transfers between devices, within(): return lax.ppermute(value, 'inner', [(i ^ step, i) for i in range(n_inner)])  3.52 us
    ppermute x2, waiting for transfers between devices, within(): return lax.ppermute(value, 'inner', [(i ^ step, i) for i in range(n_inner)])  3.29 us
    ppermute x5, waiting for transfers between devices, direct(): return lax.ppermute(value, ('outer', 'inner'), pairs)  1.7 us
    pallas_call x1, Pallas kernels, body(): pl.pallas_call(functools.partial(mix_kernel, stages, v_at, kv_heads, grou...  1.14 us
    pallas_call x3, Pallas kernels, body(): pl.pallas_call(functools.partial(weigh_kernel, stages, at, n_inner, len(n...  0.94 us
  transfers between devices with their start and end apart: 7, of which 4 were waited for; matrix products, arithmetic and copies ran while one was open for 0% of the time, Pallas kernels for 5%

profile of v3, /device:TPU:0, one launch (start us, length us, event | category | flops | bytes accessed | tf_op | source)
XLA Modules:
  0.0 18.5 jit_solution(11943429315750796150)
XLA Ops:
  0.6 2.5 %collective-permute-start.5 = (bf16[128,512]{1,0:T(8,128)(2,1)}, bf16[128,512]{1,0:T(8,128)(2,1)S(1)}, u32[]{:S(2)}, u32[]{:S(2)}) collective-permute-start(bf16[128,512]{1,0:T(8,128)(2,1)} %param.9), channel_id=1, source_target_pairs={{2,4},{3,5},{0,6},{1,7},{6,8},{7,9},{4,10},{5,11},{10,12},{11,13},... | collective-permute-start | bytes 393224 | tf_op jit(solution)/shard_map/ppermute | solution.py:253
  3.1 1.7 %collective-permute-start.4 = (bf16[128,512]{1,0:T(8,128)(2,1)}, bf16[128,512]{1,0:T(8,128)(2,1)S(1)}, u32[]{:S(2)}, u32[]{:S(2)}) collective-permute-start(bf16[128,512]{1,0:T(8,128)(2,1)} %param.9), channel_id=1, source_target_pairs={{0,4},{1,5},{2,6},{3,7},{4,8},{5,9},{6,10},{7,11},{8,12},{9,13},{1... | collective-permute-start | bytes 393224 | tf_op jit(solution)/shard_map/ppermute | solution.py:253
  4.8 1.1 %collective-permute-start.1 = (bf16[128,512]{1,0:T(8,128)(2,1)}, bf16[128,512]{1,0:T(8,128)(2,1)S(1)}, u32[]{:S(2)}, u32[]{:S(2)}) collective-permute-start(bf16[128,512]{1,0:T(8,128)(2,1)} %param.8), channel_id=1, source_target_pairs={{1,4},{0,5},{3,6},{2,7},{5,8},{4,9},{7,10},{6,11},{9,12},{8,13},{1... | collective-permute-start | bytes 393224 | tf_op jit(solution)/shard_map/ppermute | solution.py:253
  5.9 1.5 %collective-permute-start = (bf16[128,512]{1,0:T(8,128)(2,1)}, bf16[128,512]{1,0:T(8,128)(2,1)S(1)}, u32[]{:S(2)}, u32[]{:S(2)}) collective-permute-start(bf16[128,512]{1,0:T(8,128)(2,1)} %param.8), channel_id=1, source_target_pairs={{0,4},{1,5},{2,6},{3,7},{4,8},{5,9},{6,10},{7,11},{8,12},{9,13},{1... | collective-permute-start | bytes 393224 | tf_op jit(solution)/shard_map/ppermute | solution.py:253
  7.4 0.4 %collective-permute-start.2 = (bf16[128,512]{1,0:T(8,128)(2,1)}, bf16[128,512]{1,0:T(8,128)(2,1)S(1)}, u32[]{:S(2)}, u32[]{:S(2)}) collective-permute-start(bf16[128,512]{1,0:T(8,128)(2,1)} %param.8), channel_id=1, source_target_pairs={{2,4},{3,5},{0,6},{1,7},{6,8},{7,9},{4,10},{5,11},{10,12},{11,13},... | collective-permute-start | bytes 393224 | tf_op jit(solution)/shard_map/ppermute | solution.py:253
  7.8 0.2 %collective-permute-done.5.refs_11_ = bf16[128,512]{1,0:T(8,128)(2,1)S(1)} collective-permute-done((bf16[128,512]{1,0:T(8,128)(2,1)}, bf16[128,512]{1,0:T(8,128)(2,1)S(1)}, u32[]{:S(2)}, u32[]{:S(2)}) %collective-permute-start.5) | collective-permute-done | bytes 131104 | tf_op jit(solution)/shard_map/ppermute | solution.py:253
  8.0 1.5 %collective-permute-done.4.refs_9_ = bf16[128,512]{1,0:T(8,128)(2,1)S(1)} collective-permute-done((bf16[128,512]{1,0:T(8,128)(2,1)}, bf16[128,512]{1,0:T(8,128)(2,1)S(1)}, u32[]{:S(2)}, u32[]{:S(2)}) %collective-permute-start.4) | collective-permute-done | bytes 131104 | tf_op jit(solution)/shard_map/ppermute | solution.py:253
  9.5 0.0 copy-start
  9.5 0.0 copy-start.1
  9.5 0.0 copy-start.2
  9.5 0.0 copy-start.3
  9.6 0.0 copy-start.4
  9.6 2.0 %collective-permute-start.6 = (bf16[256,512]{1,0:T(8,128)(2,1)S(1)}, bf16[256,512]{1,0:T(8,128)(2,1)S(1)}, u32[]{:S(2)}, u32[]{:S(2)}) collective-permute-start(bf16[256,512]{1,0:T(8,128)(2,1)S(1)} %pad_maximum_fusion), channel_id=1, source_target_pairs={{1,0},{0,1},{3,2},{2,3},{5,4},{4,5},{7,6},{6,7},{9,8},{8,9},{11,10... | collective-permute-start | bytes 786440 | tf_op jit(solution)/shard_map/ppermute | solution.py:256
  11.6 0.0 collective-permute-done.1.refs_7_
  11.6 1.5 %collective-permute-start.3 = (bf16[128,512]{1,0:T(8,128)(2,1)S(1)}, bf16[128,512]{1,0:T(8,128)(2,1)S(1)}, u32[]{:S(2)}, u32[]{:S(2)}) collective-permute-start(bf16[128,512]{1,0:T(8,128)(2,1)S(1)} %collective-permute-done.1.refs_7_), channel_id=1, source_target_pairs={{2,0},{3,1},{0,2},{1,3},{6,4},{7,5},{4,6},{5,7},{10,8},{11,9},{8,1... | collective-permute-start | bytes 393224 | tf_op jit(solution)/shard_map/ppermute | solution.py:256
  13.1 0.0 collective-permute-done.refs_6_
  13.1 0.0 copy-done
  13.1 0.0 copy-done.1
  13.1 0.0 copy-done.2
  13.1 0.0 copy-done.3
  13.1 0.0 copy-done.4
  13.1 0.9 %shard_map.95 = (bf16[256,4096]{1,0:T(8,128)(2,1)S(1)}, f32[32,128]{1,0:T(8,128)S(1)}, f32[32,128]{1,0:T(8,128)S(1)}, f32[4096,128]{1,0:T(8,128)S(1)}, bf16[128,...) custom-call(s32[16]{0:T(128)S(1)} %copy-done.4, f32[8,128]{1,0:T(8,128)S(1)} %shard_map.94.refs_1_, ...), custom_call_target="tpu_custom_call" | custom-call | flops 268435456 | bytes 1048576 | tf_op jit(solution)/shard_map/pallas_call | solution.py:335
  14.0 0.0 collective-permute-done.2.refs_5_
  14.1 2.5 %collective-permute-done.3.refs_5_ = bf16[128,512]{1,0:T(8,128)(2,1)S(1)} collective-permute-done((bf16[128,512]{1,0:T(8,128)(2,1)S(1)}, bf16[128,512]{1,0:T(8,128)(2,1)S(1)}, u32[]{:S(2)}, u32[]{:S(2)}) %collective-permute-start.3) | collective-permute-done | bytes 131104 | tf_op jit(solution)/shard_map/ppermute | solution.py:256
  16.6 0.8 %collective-permute-done.6.refs_10_ = bf16[256,512]{1,0:T(8,128)(2,1)S(1)} collective-permute-done((bf16[256,512]{1,0:T(8,128)(2,1)S(1)}, bf16[256,512]{1,0:T(8,128)(2,1)S(1)}, u32[]{:S(2)}, u32[]{:S(2)}) %collective-permute-start.6) | collective-permute-done | bytes 262176 | tf_op jit(solution)/shard_map/ppermute | solution.py:256
  17.4 1.1 %shard_map.98 = (bf16[128,4096]{1,0:T(8,128)(2,1)}, f32[32,128]{1,0:T(8,128)}, f32[32,128]{1,0:T(8,128)}) custom-call(f32[32,128]{1,0:T(8,128)S(1)} %get-tuple-element.29.refs_0_, f32[32,128]{1,0:T(8,128)S(1)} %get-tuple-element.30.refs_1_, bf16[256,4096]{1,0:T(8,128)(2,1)S(1)} %get-tuple-element.31.refs_2_, ...), custom_call_target="tpu_custom_call" | custom-call | flops 536870912 | bytes 1048576 | tf_op jit(solution)/shard_map/pallas_call | solution.py:371
  (4 shorter events, 0.1 us)
Async XLA Ops:
  0.6 7.4 %collective-permute-start.5 = (bf16[128,512]{1,0:T(8,128)(2,1)}, bf16[128,512]{1,0:T(8,128)(2,1)S(1)}, u32[]{:S(2)}, u32[]{:S(2)}) collective-permute-start(bf16[128,512]{1,0:T(8,128)(2,1)} %param.9), channel_id=1, source_target_pairs={{2,4},{3,5},{0,6},{1,7},{6,8},{7,9},{4,10},{5,11},{10,12},{11,13},... | collective-permute-start | bytes 393224 | tf_op jit(solution)/shard_map/ppermute | solution.py:253
  3.1 6.4 %collective-permute-start.4 = (bf16[128,512]{1,0:T(8,128)(2,1)}, bf16[128,512]{1,0:T(8,128)(2,1)S(1)}, u32[]{:S(2)}, u32[]{:S(2)}) collective-permute-start(bf16[128,512]{1,0:T(8,128)(2,1)} %param.9), channel_id=1, source_target_pairs={{0,4},{1,5},{2,6},{3,7},{4,8},{5,9},{6,10},{7,11},{8,12},{9,13},{1... | collective-permute-start | bytes 393224 | tf_op jit(solution)/shard_map/ppermute | solution.py:253
  4.8 6.8 %collective-permute-start.1 = (bf16[128,512]{1,0:T(8,128)(2,1)}, bf16[128,512]{1,0:T(8,128)(2,1)S(1)}, u32[]{:S(2)}, u32[]{:S(2)}) collective-permute-start(bf16[128,512]{1,0:T(8,128)(2,1)} %param.8), channel_id=1, source_target_pairs={{1,4},{0,5},{3,6},{2,7},{5,8},{4,9},{7,10},{6,11},{9,12},{8,13},{1... | collective-permute-start | bytes 393224 | tf_op jit(solution)/shard_map/ppermute | solution.py:253
  5.9 7.2 %collective-permute-start = (bf16[128,512]{1,0:T(8,128)(2,1)}, bf16[128,512]{1,0:T(8,128)(2,1)S(1)}, u32[]{:S(2)}, u32[]{:S(2)}) collective-permute-start(bf16[128,512]{1,0:T(8,128)(2,1)} %param.8), channel_id=1, source_target_pairs={{0,4},{1,5},{2,6},{3,7},{4,8},{5,9},{6,10},{7,11},{8,12},{9,13},{1... | collective-permute-start | bytes 393224 | tf_op jit(solution)/shard_map/ppermute | solution.py:253
  7.4 6.6 %collective-permute-start.2 = (bf16[128,512]{1,0:T(8,128)(2,1)}, bf16[128,512]{1,0:T(8,128)(2,1)S(1)}, u32[]{:S(2)}, u32[]{:S(2)}) collective-permute-start(bf16[128,512]{1,0:T(8,128)(2,1)} %param.8), channel_id=1, source_target_pairs={{2,4},{3,5},{0,6},{1,7},{6,8},{7,9},{4,10},{5,11},{10,12},{11,13},... | collective-permute-start | bytes 393224 | tf_op jit(solution)/shard_map/ppermute | solution.py:253
  9.5 3.6 %copy-start = (bf16[128,4096]{1,0:T(8,128)(2,1)S(1)}, bf16[128,4096]{1,0:T(8,128)(2,1)}, u32[]{:S(2)}) copy-start(bf16[128,4096]{1,0:T(8,128)(2,1)} %refs_2_.5) | copy-start | bytes 3145732
  9.5 3.6 %copy-start.1 = (bf16[128,4096]{1,0:T(8,128)(2,1)S(1)}, bf16[128,4096]{1,0:T(8,128)(2,1)}, u32[]{:S(2)}) copy-start(bf16[128,4096]{1,0:T(8,128)(2,1)} %refs_2_.3) | copy-start | bytes 3145732
  9.5 3.6 %copy-start.2 = (f32[128,32]{0,1:T(8,128)S(1)}, f32[128,32]{0,1:T(8,128)}, u32[]{:S(2)}) copy-start(f32[128,32]{0,1:T(8,128)} %param.11) | copy-start | bytes 49156
  9.5 3.6 %copy-start.3 = (f32[128,32]{0,1:T(8,128)S(1)}, f32[128,32]{0,1:T(8,128)}, u32[]{:S(2)}) copy-start(f32[128,32]{0,1:T(8,128)} %param.12) | copy-start | bytes 49156
  9.6 3.6 %copy-start.4 = (s32[16]{0:T(128)S(1)}, s32[16]{0:T(128)}, u32[]{:S(2)}) copy-start(s32[16]{0:T(128)} %refs_0_.1) | copy-start | bytes 196
  9.6 7.8 %collective-permute-start.6 = (bf16[256,512]{1,0:T(8,128)(2,1)S(1)}, bf16[256,512]{1,0:T(8,128)(2,1)S(1)}, u32[]{:S(2)}, u32[]{:S(2)}) collective-permute-start(bf16[256,512]{1,0:T(8,128)(2,1)S(1)} %pad_maximum_fusion), channel_id=1, source_target_pairs={{1,0},{0,1},{3,2},{2,3},{5,4},{4,5},{7,6},{6,7},{9,8},{8,9},{11,10... | collective-permute-start | bytes 786440 | tf_op jit(solution)/shard_map/ppermute | solution.py:256
  11.6 5.0 %collective-permute-start.3 = (bf16[128,512]{1,0:T(8,128)(2,1)S(1)}, bf16[128,512]{1,0:T(8,128)(2,1)S(1)}, u32[]{:S(2)}, u32[]{:S(2)}) collective-permute-start(bf16[128,512]{1,0:T(8,128)(2,1)S(1)} %collective-permute-done.1.refs_7_), channel_id=1, source_target_pairs={{2,0},{3,1},{0,2},{1,3},{6,4},{7,5},{4,6},{5,7},{10,8},{11,9},{8,1... | collective-permute-start | bytes 393224 | tf_op jit(solution)/shard_map/ppermute | solution.py:256

commit v4 on v3

--- a/solution.py
+++ b/solution.py
@@ -75,8 +75,8 @@
     refs = list(refs)
     if begin:
         doc_ref, unused, old_ref = refs[:3]
-        mine_ref, hide_ref = refs[-2:]
-        refs = refs[3:-2]
+        mine_ref, hide_ref = refs[-3:-1]
+        refs = refs[3:-3] + refs[-1:]
     else:
         mine_ref, hide_ref = refs[:2]
         refs = refs[2:]
@@ -92,7 +92,8 @@
     if not begin:
         shrink_ref = refs.pop(0)
     if begin:
-        acc_ref = refs.pop(0)
+        acc_ref, *rest_refs = refs[:4]
+        rest_sems, refs = refs[-1], refs[4:-1]
         if len(stages) > 1:
             later_mine_ref, later_refs = refs[0], refs[1:]
     split = early * rows
@@ -161,24 +162,30 @@
 
     @pl.when(jnp.logical_not(live))
     def _():
-        for h, heads in work:
-            total = rows_of(sum_ref, heads)
-            numer = old_of(heads) * total if begin else None
-            finish(heads, rows_of(max_ref, heads), total, jnp.ones_like(total), numer)
+        if begin:
+            copies = [
+                pltpu.make_async_copy(ref, rest, rest_sems.at[n])
+                for n, (ref, rest) in enumerate(zip((old_ref, max_ref, sum_ref), rest_refs))
+            ]
+            for copy in copies:
+                copy.start()
+        top_ref[...] = max_ref[...]
+        total_ref[...] = sum_ref[...]
+        if begin:
+            for copy in copies:
+                copy.wait()
 
 
 def mix_kernel(stages, v_at, kv_heads, group, *refs):
     out_ref, top_out, total_out, stage, sems, stat_sems = refs[-6:]
-    top_ref, total_ref = refs[:2]
-    refs = refs[2:]
+    top_ref, total_ref = refs[3:5]
+    refs = refs[5:]
     rows = out_ref.shape[0]
     count = len(v_at)
     stats = [
         pltpu.make_async_copy(top_ref, top_out, stat_sems.at[0]),
         pltpu.make_async_copy(total_ref, total_out, stat_sems.at[1]),
     ]
-    for copy in stats:
-        copy.start()
     w_refs, shrink_refs = refs[:count], refs[count : 2 * count - 1]
     acc_ref, inverse_ref = refs[2 * count - 1 : 2 * count + 1]
     refs = refs[2 * count + 1 :]
@@ -200,10 +207,10 @@
     def numer_of(heads):
         return jnp.concatenate([acc_ref[pl.ds(x * HD, HD), :] for x in heads], axis=1)
 
-    live = lax.axis_index("outer") > 0
-
-    @pl.when(live)
+    @pl.when(lax.axis_index("outer") > 0)
     def _():
+        for copy in stats:
+            copy.start()
         vals = {}
 
         def mixed(h, heads):
@@ -232,15 +239,10 @@
             if t >= 1:
                 close(work[t - 1][1], held.pop(t - 1))
 
-    @pl.when(jnp.logical_not(live))
-    def _():
-        for h, heads in work:
-            finish(heads, numer_of(heads))
-
-    for h in range(kv_heads * group // FLUSH):
-        flush(h).wait()
-    for copy in stats:
-        copy.wait()
+        for h in range(kv_heads * group // FLUSH):
+            flush(h).wait()
+        for copy in stats:
+            copy.wait()
 
 
 def move(keys, values, n_outer, n_inner):
@@ -329,8 +331,11 @@
         operands += [queries, top, total, *arrays]
         out_shape = [jax.ShapeDtypeStruct((max(1, len(late[-1])) * rows, heads * rows), jnp.bfloat16), stat, stat]
         out_shape += [stat] * ((not begin) + end)
+        out_specs = [VMEM] * len(out_shape)
         if begin:
             out_shape.append(jax.ShapeDtypeStruct((width, rows), jnp.float32))
+            out_shape += [jax.ShapeDtypeStruct((rows, width), jnp.bfloat16), stat, stat]
+            out_specs += [VMEM] + [pl.BlockSpec(memory_space=pl.ANY)] * 3
             out_shape += [tile] + [hide_of(steps) for steps in stages[1:]] if not end else []
         outs = pl.pallas_call(
             functools.partial(
@@ -347,8 +352,10 @@
             ),
             out_shape=tuple(out_shape),
             in_specs=([SMEM] if begin else [VMEM]) + [VMEM] * (len(operands) - 1),
-            out_specs=(VMEM,) * len(out_shape),
-            scratch_shapes=[pltpu.VMEM(x.shape, x.dtype) for x in (tile, hide_of(steps))] if begin else [],
+            out_specs=tuple(out_specs + [VMEM] * (len(out_shape) - len(out_specs))),
+            scratch_shapes=[pltpu.VMEM(x.shape, x.dtype) for x in (tile, hide_of(steps))] + [pltpu.SemaphoreType.DMA((3,))]
+            if begin
+            else [],
             compiler_params=pltpu.CompilerParams(vmem_limit_bytes=12 * 2**20),
             cost_estimate=pl.CostEstimate(
                 flops=2 * area * HD * (len(steps) + len(now)), bytes_accessed=2**20, transcendentals=area * len(steps)
@@ -363,7 +370,7 @@
         if not begin:
             shrinks.append(outs.pop(0))
         else:
-            acc = outs.pop(0)
+            acc, rest, outs = outs[0], outs[1:4], outs[4:]
             mine, hides = (outs[0], outs[1:]) if not end else (None, None)
     arrays, places = gather(got, [f"{step}v" for held in late for step in held])
     places = iter(places)
@@ -371,7 +378,8 @@
     out, top, total = pl.pallas_call(
         functools.partial(mix_kernel, stages, v_at, kv_heads, group),
         out_shape=(jax.ShapeDtypeStruct((rows, width), jnp.bfloat16), stat, stat),
-        in_specs=[VMEM] * (2 * len(stages) + 3 + len(arrays)),
+        in_specs=[pl.BlockSpec(memory_space=pl.ANY)] * 3 + [VMEM] * (2 * len(stages) + 3 + len(arrays)),
+        input_output_aliases={0: 0, 1: 1, 2: 2},
         out_specs=(pl.BlockSpec(memory_space=pl.ANY),) * 3,
         scratch_shapes=[
             pltpu.VMEM((rows, width), jnp.bfloat16),
@@ -380,7 +388,7 @@
         ],
         compiler_params=pltpu.CompilerParams(vmem_limit_bytes=12 * 2**20),
         cost_estimate=pl.CostEstimate(flops=2 * area * HD * n_inner, bytes_accessed=2**20, transcendentals=0),
-    )(top, total, *ws, *shrinks, acc, inverse, *arrays)
+    )(*rest, top, total, *ws, *shrinks, acc, inverse, *arrays)
     return out, top.T, total.T
 
 

time: 18.7 us -> 18.2 us (0.973)
  the two profiles are of different devices: /device:TPU:0 before, /device:TPU:8 now
where the time goes in v4:
time: 18.2 us; the launch traced here: 18 us
  starting transfers between devices  7.76 us (43%)
  Pallas kernels  6.18 us (34%)
  waiting for transfers between devices  3.28 us (18%)
  between operations  0.74 us (4%)
    ppermute x5, starting transfers between devices, direct(): return lax.ppermute(value, ('outer', 'inner'), pairs)  5.72 us
    pallas_call x3, Pallas kernels, body(): pl.pallas_call(functools.partial(weigh_kernel, stages, at, n_inner, len(n...  4.18 us
    ppermute x5, waiting for transfers between devices, direct(): return lax.ppermute(value, ('outer', 'inner'), pairs)  2.08 us
    ppermute x2, starting transfers between devices, within(): return lax.ppermute(value, 'inner', [(i ^ step, i) for i in range(n_inner)])  2.03 us
    pallas_call x1, Pallas kernels, body(): pl.pallas_call(functools.partial(mix_kernel, stages, v_at, kv_heads, grou...  2 us
    ppermute x2, waiting for transfers between devices, within(): return lax.ppermute(value, 'inner', [(i ^ step, i) for i in range(n_inner)])  1.21 us
  transfers between devices with their start and end apart: 7, of which 3 were waited for; matrix products, arithmetic and copies ran while one was open for 0% of the time, Pallas kernels for 23%

profile of v4, /device:TPU:8, one launch (start us, length us, event | category | flops | bytes accessed | tf_op | source)
XLA Modules:
  0.0 18.0 jit_solution(4434301689308027376)
XLA Ops:
  0.6 1.0 %collective-permute-start.5 = (bf16[128,512]{1,0:T(8,128)(2,1)}, bf16[128,512]{1,0:T(8,128)(2,1)S(1)}, u32[]{:S(2)}, u32[]{:S(2)}) collective-permute-start(bf16[128,512]{1,0:T(8,128)(2,1)} %param.9), channel_id=1, source_target_pairs={{2,4},{3,5},{0,6},{1,7},{6,8},{7,9},{4,10},{5,11},{10,12},{11,13},... | collective-permute-start | bytes 393224 | tf_op jit(solution)/shard_map/ppermute | solution.py:255
  1.6 1.7 %collective-permute-start.4 = (bf16[128,512]{1,0:T(8,128)(2,1)}, bf16[128,512]{1,0:T(8,128)(2,1)S(1)}, u32[]{:S(2)}, u32[]{:S(2)}) collective-permute-start(bf16[128,512]{1,0:T(8,128)(2,1)} %param.9), channel_id=1, source_target_pairs={{0,4},{1,5},{2,6},{3,7},{4,8},{5,9},{6,10},{7,11},{8,12},{9,13},{1... | collective-permute-start | bytes 393224 | tf_op jit(solution)/shard_map/ppermute | solution.py:255
  3.3 1.1 %collective-permute-start.1 = (bf16[128,512]{1,0:T(8,128)(2,1)}, bf16[128,512]{1,0:T(8,128)(2,1)S(1)}, u32[]{:S(2)}, u32[]{:S(2)}) collective-permute-start(bf16[128,512]{1,0:T(8,128)(2,1)} %param.8), channel_id=1, source_target_pairs={{1,4},{0,5},{3,6},{2,7},{5,8},{4,9},{7,10},{6,11},{9,12},{8,13},{1... | collective-permute-start | bytes 393224 | tf_op jit(solution)/shard_map/ppermute | solution.py:255
  4.4 1.5 %collective-permute-start = (bf16[128,512]{1,0:T(8,128)(2,1)}, bf16[128,512]{1,0:T(8,128)(2,1)S(1)}, u32[]{:S(2)}, u32[]{:S(2)}) collective-permute-start(bf16[128,512]{1,0:T(8,128)(2,1)} %param.8), channel_id=1, source_target_pairs={{0,4},{1,5},{2,6},{3,7},{4,8},{5,9},{6,10},{7,11},{8,12},{9,13},{1... | collective-permute-start | bytes 393224 | tf_op jit(solution)/shard_map/ppermute | solution.py:255
  6.0 0.4 %collective-permute-start.2 = (bf16[128,512]{1,0:T(8,128)(2,1)}, bf16[128,512]{1,0:T(8,128)(2,1)S(1)}, u32[]{:S(2)}, u32[]{:S(2)}) collective-permute-start(bf16[128,512]{1,0:T(8,128)(2,1)} %param.8), channel_id=1, source_target_pairs={{2,4},{3,5},{0,6},{1,7},{6,8},{7,9},{4,10},{5,11},{10,12},{11,13},... | collective-permute-start | bytes 393224 | tf_op jit(solution)/shard_map/ppermute | solution.py:255
  6.4 0.0 collective-permute-done.5.refs_14_
  6.4 1.3 %collective-permute-done.4.refs_12_ = bf16[128,512]{1,0:T(8,128)(2,1)S(1)} collective-permute-done((bf16[128,512]{1,0:T(8,128)(2,1)}, bf16[128,512]{1,0:T(8,128)(2,1)S(1)}, u32[]{:S(2)}, u32[]{:S(2)}) %collective-permute-start.4) | collective-permute-done | bytes 131104 | tf_op jit(solution)/shard_map/ppermute | solution.py:255
  7.7 0.0 copy-start
  7.7 0.0 copy-start.1
  7.7 0.0 copy-start.2
  7.8 0.0 copy-start.3
  7.8 0.0 copy-start.4
  7.8 1.6 %collective-permute-start.6 = (bf16[256,512]{1,0:T(8,128)(2,1)S(1)}, bf16[256,512]{1,0:T(8,128)(2,1)S(1)}, u32[]{:S(2)}, u32[]{:S(2)}) collective-permute-start(bf16[256,512]{1,0:T(8,128)(2,1)S(1)} %pad_maximum_fusion), channel_id=1, source_target_pairs={{1,0},{0,1},{3,2},{2,3},{5,4},{4,5},{7,6},{6,7},{9,8},{8,9},{11,10... | collective-permute-start | bytes 786440 | tf_op jit(solution)/shard_map/ppermute | solution.py:258
  9.3 0.7 %collective-permute-done.1.refs_7_ = bf16[128,512]{1,0:T(8,128)(2,1)S(1)} collective-permute-done((bf16[128,512]{1,0:T(8,128)(2,1)}, bf16[128,512]{1,0:T(8,128)(2,1)S(1)}, u32[]{:S(2)}, u32[]{:S(2)}) %collective-permute-start.1) | collective-permute-done | bytes 131104 | tf_op jit(solution)/shard_map/ppermute | solution.py:255
  10.1 0.5 %collective-permute-start.3 = (bf16[128,512]{1,0:T(8,128)(2,1)S(1)}, bf16[128,512]{1,0:T(8,128)(2,1)S(1)}, u32[]{:S(2)}, u32[]{:S(2)}) collective-permute-start(bf16[128,512]{1,0:T(8,128)(2,1)S(1)} %collective-permute-done.1.refs_7_), channel_id=1, source_target_pairs={{2,0},{3,1},{0,2},{1,3},{6,4},{7,5},{4,6},{5,7},{10,8},{11,9},{8,1... | collective-permute-start | bytes 393224 | tf_op jit(solution)/shard_map/ppermute | solution.py:258
  10.5 0.0 collective-permute-done.refs_6_
  10.5 0.0 copy-done
  10.6 0.0 copy-done.1
  10.6 0.0 copy-done.2
  10.6 0.0 copy-done.3
  10.6 0.0 copy-done.4
  10.6 2.4 %shard_map.95 = (bf16[256,4096]{1,0:T(8,128)(2,1)S(1)}, f32[32,128]{1,0:T(8,128)S(1)}, f32[32,128]{1,0:T(8,128)S(1)}, f32[4096,128]{1,0:T(8,128)S(1)}, bf16[128,...) custom-call(s32[16]{0:T(128)S(1)} %copy-done.4, ...), custom_call_target="tpu_custom_call" | custom-call | flops 268435456 | bytes 1048576 | tf_op jit(solution)/shard_map/pallas_call | solution.py:340
  13.0 0.0 collective-permute-done.2.refs_5_
  13.0 0.9 %shard_map.96 = (bf16[128,4096]{1,0:T(8,128)(2,1)S(1)}, f32[32,128]{1,0:T(8,128)S(1)}, f32[32,128]{1,0:T(8,128)S(1)}, f32[32,128]{1,0:T(8,128)S(1)}) custom-call(bf16[128,128]{1,0:T(8,128)(2,1)S(1)} %get-tuple-element.28.refs_0_, bf16[128,128]{1,0:T(8,128)(2,1)S(1)} %get-tuple-element.30.refs_1_, bf16[128,4096]{1,0:T(8,128)(2,1)S(1)} %copy-done, ...), custom_call_target="tpu_custom_call" | custom-call | flops 134217728 | bytes 1048576 | tf_op jit(solution)/shard_map/pallas_call | solution.py:340
  13.9 1.2 %collective-permute-done.3.refs_5_ = bf16[128,512]{1,0:T(8,128)(2,1)S(1)} collective-permute-done((bf16[128,512]{1,0:T(8,128)(2,1)S(1)}, bf16[128,512]{1,0:T(8,128)(2,1)S(1)}, u32[]{:S(2)}, u32[]{:S(2)}) %collective-permute-start.3) | collective-permute-done | bytes 131104 | tf_op jit(solution)/shard_map/ppermute | solution.py:258
  15.1 0.9 %shard_map.97 = (bf16[128,4096]{1,0:T(8,128)(2,1)S(1)}, f32[32,128]{1,0:T(8,128)S(1)}, f32[32,128]{1,0:T(8,128)S(1)}, f32[32,128]{1,0:T(8,128)S(1)}, f32[32,128]{1,0:T(8,128)S(1)}) custom-call(bf16[128,128]{1,0:T(8,128)(2,1)S(1)} %get-tuple-element.28.refs_0_, bf16[128,128]{1,0:T(8,128)(2,1)S(1)} %get-tuple-element.29.refs_1_, ...), custom_call_target="tpu_custom_call" | custom-call | flops 134217728 | bytes 1048576 | tf_op jit(solution)/shard_map/pallas_call | solution.py:340
  16.0 0.0 collective-permute-done.6.refs_13_
  16.0 2.0 %shard_map.98 = (bf16[128,4096]{1,0:T(8,128)(2,1)}, f32[32,128]{1,0:T(8,128)}, f32[32,128]{1,0:T(8,128)}) custom-call(bf16[128,4096]{1,0:T(8,128)(2,1)} %get-tuple-element.25.refs_0_, f32[32,128]{1,0:T(8,128)} %get-tuple-element.26.refs_1_, f32[32,128]{1,0:T(8,128)} %get-tuple-element.27.refs_2_, ...), custom_call_target="tpu_custom_call", output_to_operand_aliasing={{0}: (0, {}), {1}: (1, {}), {2}: (2, {})} | custom-call | flops 536870912 | bytes 1048576 | tf_op jit(solution)/shard_map/pallas_call | solution.py:378
  (2 shorter events, 0.0 us)
Async XLA Ops:
  0.6 5.7 %collective-permute-start.5 = (bf16[128,512]{1,0:T(8,128)(2,1)}, bf16[128,512]{1,0:T(8,128)(2,1)S(1)}, u32[]{:S(2)}, u32[]{:S(2)}) collective-permute-start(bf16[128,512]{1,0:T(8,128)(2,1)} %param.9), channel_id=1, source_target_pairs={{2,4},{3,5},{0,6},{1,7},{6,8},{7,9},{4,10},{5,11},{10,12},{11,13},... | collective-permute-start | bytes 393224 | tf_op jit(solution)/shard_map/ppermute | solution.py:255
  1.6 6.1 %collective-permute-start.4 = (bf16[128,512]{1,0:T(8,128)(2,1)}, bf16[128,512]{1,0:T(8,128)(2,1)S(1)}, u32[]{:S(2)}, u32[]{:S(2)}) collective-permute-start(bf16[128,512]{1,0:T(8,128)(2,1)} %param.9), channel_id=1, source_target_pairs={{0,4},{1,5},{2,6},{3,7},{4,8},{5,9},{6,10},{7,11},{8,12},{9,13},{1... | collective-permute-start | bytes 393224 | tf_op jit(solution)/shard_map/ppermute | solution.py:255
  3.3 6.7 %collective-permute-start.1 = (bf16[128,512]{1,0:T(8,128)(2,1)}, bf16[128,512]{1,0:T(8,128)(2,1)S(1)}, u32[]{:S(2)}, u32[]{:S(2)}) collective-permute-start(bf16[128,512]{1,0:T(8,128)(2,1)} %param.8), channel_id=1, source_target_pairs={{1,4},{0,5},{3,6},{2,7},{5,8},{4,9},{7,10},{6,11},{9,12},{8,13},{1... | collective-permute-start | bytes 393224 | tf_op jit(solution)/shard_map/ppermute | solution.py:255
  4.4 6.1 %collective-permute-start = (bf16[128,512]{1,0:T(8,128)(2,1)}, bf16[128,512]{1,0:T(8,128)(2,1)S(1)}, u32[]{:S(2)}, u32[]{:S(2)}) collective-permute-start(bf16[128,512]{1,0:T(8,128)(2,1)} %param.8), channel_id=1, source_target_pairs={{0,4},{1,5},{2,6},{3,7},{4,8},{5,9},{6,10},{7,11},{8,12},{9,13},{1... | collective-permute-start | bytes 393224 | tf_op jit(solution)/shard_map/ppermute | solution.py:255
  6.0 7.1 %collective-permute-start.2 = (bf16[128,512]{1,0:T(8,128)(2,1)}, bf16[128,512]{1,0:T(8,128)(2,1)S(1)}, u32[]{:S(2)}, u32[]{:S(2)}) collective-permute-start(bf16[128,512]{1,0:T(8,128)(2,1)} %param.8), channel_id=1, source_target_pairs={{2,4},{3,5},{0,6},{1,7},{6,8},{7,9},{4,10},{5,11},{10,12},{11,13},... | collective-permute-start | bytes 393224 | tf_op jit(solution)/shard_map/ppermute | solution.py:255
  7.7 2.8 %copy-start = (bf16[128,4096]{1,0:T(8,128)(2,1)S(1)}, bf16[128,4096]{1,0:T(8,128)(2,1)}, u32[]{:S(2)}) copy-start(bf16[128,4096]{1,0:T(8,128)(2,1)} %refs_2_.5) | copy-start | bytes 3145732
  7.7 2.8 %copy-start.1 = (bf16[128,4096]{1,0:T(8,128)(2,1)S(1)}, bf16[128,4096]{1,0:T(8,128)(2,1)}, u32[]{:S(2)}) copy-start(bf16[128,4096]{1,0:T(8,128)(2,1)} %refs_2_.3) | copy-start | bytes 3145732
  7.7 2.8 %copy-start.2 = (f32[128,32]{0,1:T(8,128)S(1)}, f32[128,32]{0,1:T(8,128)}, u32[]{:S(2)}) copy-start(f32[128,32]{0,1:T(8,128)} %param.11) | copy-start | bytes 49156
  7.8 2.8 %copy-start.3 = (f32[128,32]{0,1:T(8,128)S(1)}, f32[128,32]{0,1:T(8,128)}, u32[]{:S(2)}) copy-start(f32[128,32]{0,1:T(8,128)} %param.12) | copy-start | bytes 49156
  7.8 2.8 %copy-start.4 = (s32[16]{0:T(128)S(1)}, s32[16]{0:T(128)}, u32[]{:S(2)}) copy-start(s32[16]{0:T(128)} %refs_0_.1) | copy-start | bytes 196
  7.8 8.2 %collective-permute-start.6 = (bf16[256,512]{1,0:T(8,128)(2,1)S(1)}, bf16[256,512]{1,0:T(8,128)(2,1)S(1)}, u32[]{:S(2)}, u32[]{:S(2)}) collective-permute-start(bf16[256,512]{1,0:T(8,128)(2,1)S(1)} %pad_maximum_fusion), channel_id=1, source_target_pairs={{1,0},{0,1},{3,2},{2,3},{5,4},{4,5},{7,6},{6,7},{9,8},{8,9},{11,10... | collective-permute-start | bytes 786440 | tf_op jit(solution)/shard_map/ppermute | solution.py:258
  10.1 5.1 %collective-permute-start.3 = (bf16[128,512]{1,0:T(8,128)(2,1)S(1)}, bf16[128,512]{1,0:T(8,128)(2,1)S(1)}, u32[]{:S(2)}, u32[]{:S(2)}) collective-permute-start(bf16[128,512]{1,0:T(8,128)(2,1)S(1)} %collective-permute-done.1.refs_7_), channel_id=1, source_target_pairs={{2,0},{3,1},{0,2},{1,3},{6,4},{7,5},{4,6},{5,7},{10,8},{11,9},{8,1... | collective-permute-start | bytes 393224 | tf_op jit(solution)/shard_map/ppermute | solution.py:258

commit v5 on v4

--- a/solution.py
+++ b/solution.py
@@ -15,6 +15,7 @@
 VMEM = pl.BlockSpec(memory_space=pltpu.VMEM)
 SMEM = pl.BlockSpec(memory_space=pltpu.SMEM)
 PAIR = 1
+EARLY_PAIR = 4
 MIX_PAIR = 2
 FLUSH = 8
 PLAN = (
@@ -27,7 +28,7 @@
     (("1v", "3v"), ("0v", "2v"), 1),
 )
 STAGES = ((0, 1), (2,), (3,))
-EARLY = ()
+EARLY = ((), (2,), ())
 TIES = {}
 AHEAD_FLOPS = 2 * 10**10
 
@@ -72,6 +73,7 @@
 
 def weigh_kernel(stages, at, n_inner, early, k_at, v_at, kv_heads, group, scale, *refs):
     begin, end = at == 0, at + 1 == len(stages)
+    carry = begin or early > 0
     refs = list(refs)
     if begin:
         doc_ref, unused, old_ref = refs[:3]
@@ -80,6 +82,8 @@
     else:
         mine_ref, hide_ref = refs[:2]
         refs = refs[2:]
+        if carry:
+            old_ref = refs.pop(0)
     q_ref, max_ref, sum_ref = refs[:3]
     rows = q_ref.shape[0]
     k_refs = [refs[3 + which].at[pl.ds(first, rows)] for which, first in k_at]
@@ -91,13 +95,16 @@
         inverse_ref = refs.pop(0)
     if not begin:
         shrink_ref = refs.pop(0)
+    if carry:
+        acc_ref = refs.pop(0)
     if begin:
-        acc_ref, *rest_refs = refs[:4]
-        rest_sems, refs = refs[-1], refs[4:-1]
+        rest_refs = refs[:3]
+        rest_sems, refs = refs[-1], refs[3:-1]
         if len(stages) > 1:
             later_mine_ref, later_refs = refs[0], refs[1:]
     split = early * rows
-    work = work_of(kv_heads, group, PAIR)
+    pair = EARLY_PAIR if early else PAIR
+    work = work_of(kv_heads, group, pair)
     live = lax.axis_index("outer") > 0
 
     def finish(heads, top, total, shrink, numer):
@@ -108,12 +115,14 @@
             total_ref[pl.ds(x, 1), :] = total[:, cut]
             if end:
                 inverse_ref[pl.ds(x, 1), :] = inverse[:, cut]
-            if begin:
+            if carry:
                 acc_ref[pl.ds(x * HD, HD), :] = numer[:, cut]
-            else:
+            if not begin:
                 shrink_ref[pl.ds(x, 1), :] = shrink[:, cut]
 
     def old_of(heads):
+        if not begin:
+            return jnp.concatenate([old_ref[pl.ds(x * HD, HD), :] for x in heads], axis=1)
         return jnp.concatenate([old_ref[:, pl.ds(x * HD, HD)].T for x in heads], axis=1).astype(jnp.float32)
 
     @pl.when(live)
@@ -122,7 +131,7 @@
             masks(stages, n_inner, doc_ref, mine_ref, [hide_ref] + list(later_refs if len(stages) > 1 else []))
             if len(stages) > 1:
                 later_mine_ref[...] = mine_ref[...]
-        mine = jnp.concatenate([mine_ref[...]] * PAIR, axis=0)
+        mine = jnp.concatenate([mine_ref[...]] * pair, axis=0)
         keys, vals = {}, {}
 
         def score(h, heads):
@@ -146,7 +155,7 @@
             return kept, top, total, shrink, w[:split]
 
         def mix(h, heads, kept, top, total, shrink, w):
-            numer = old_of(heads) * kept if begin else None
+            numer = old_of(heads) * (kept if begin else shrink) if carry else None
             if early:
                 numer += jnp.dot(vals[h], w, preferred_element_type=jnp.float32)
             finish(heads, top, total, shrink, numer)
@@ -176,7 +185,7 @@
                 copy.wait()
 
 
-def mix_kernel(stages, v_at, kv_heads, group, *refs):
+def mix_kernel(carried, v_at, kv_heads, group, *refs):
     out_ref, top_out, total_out, stage, sems, stat_sems = refs[-6:]
     top_ref, total_ref = refs[3:5]
     refs = refs[5:]
@@ -224,10 +233,10 @@
             ]
 
         def close(heads, parts):
-            numer = numer_of(heads)
+            numer = None
             for at, part in enumerate(parts):
-                if part is not None:
-                    numer = numer + part
+                terms = [numer, numer_of(heads) if at == carried else None, part]
+                numer = functools.reduce(lambda x, y: x + y, [term for term in terms if term is not None], jnp.float32(0.0))
                 if at + 1 < len(parts):
                     numer = numer * rows_of(shrink_refs[at], heads)
             finish(heads, numer)
@@ -255,7 +264,10 @@
         return lax.ppermute(value, ("outer", "inner"), pairs)
 
     def within(value, step):
-        return lax.ppermute(value, "inner", [(i ^ step, i) for i in range(n_inner)])
+        pairs = [
+            (o * n_inner + (i ^ (step if o else 3 - step)), o * n_inner + i) for o in range(n_outer) for i in range(n_inner)
+        ]
+        return lax.ppermute(value, ("outer", "inner"), pairs)
 
     own = {"k": keys, "v": values}
     rows = keys.shape[0]
@@ -304,7 +316,7 @@
         stages, early = STAGES, EARLY
     else:
         half = n_inner // 2
-        stages, early = (tuple(range(half)), tuple(range(half, n_inner))), ()
+        stages, early = (tuple(range(half)), tuple(range(half, n_inner))), ((), ())
     got = move(keys, values, n_outer, n_inner)
     ahead = pl.pallas_call(
         ahead_kernel,
@@ -324,23 +336,26 @@
     top, total = acc_max.T, acc_sum.T
     for at, steps in enumerate(stages):
         begin, end = at == 0, at + 1 == len(stages)
-        now = early if begin else ()
+        now = early[at]
+        carry = begin or len(now) > 0
         late.append([step for step in steps if step not in now])
-        arrays, places = gather(got, [f"{step}k" for step in steps] + [f"{step}v" for step in now])
-        operands = [doc_lengths, ahead, acc_out] if begin else [mine, hides[at - 1]]
+        order = (*now, *late[-1])
+        arrays, places = gather(got, [f"{step}k" for step in order] + [f"{step}v" for step in now])
+        operands = [doc_lengths, ahead, acc_out] if begin else [mine, hides[at - 1]] + ([acc] if carry else [])
         operands += [queries, top, total, *arrays]
         out_shape = [jax.ShapeDtypeStruct((max(1, len(late[-1])) * rows, heads * rows), jnp.bfloat16), stat, stat]
         out_shape += [stat] * ((not begin) + end)
+        if carry:
+            out_shape.append(jax.ShapeDtypeStruct((width, rows), jnp.float32))
         out_specs = [VMEM] * len(out_shape)
         if begin:
-            out_shape.append(jax.ShapeDtypeStruct((width, rows), jnp.float32))
             out_shape += [jax.ShapeDtypeStruct((rows, width), jnp.bfloat16), stat, stat]
-            out_specs += [VMEM] + [pl.BlockSpec(memory_space=pl.ANY)] * 3
-            out_shape += [tile] + [hide_of(steps) for steps in stages[1:]] if not end else []
+            out_specs += [pl.BlockSpec(memory_space=pl.ANY)] * 3
+            out_shape += [tile] + [hide_of(held) for held in stages[1:]] if not end else []
         outs = pl.pallas_call(
             functools.partial(
                 weigh_kernel,
-                stages,
+                (order, *stages[1:]) if begin else stages,
                 at,
                 n_inner,
                 len(now),
@@ -369,14 +384,16 @@
             inverse = outs.pop(0)
         if not begin:
             shrinks.append(outs.pop(0))
-        else:
-            acc, rest, outs = outs[0], outs[1:4], outs[4:]
+        if carry:
+            acc, carried = outs.pop(0), at
+        if begin:
+            rest, outs = outs[:3], outs[3:]
             mine, hides = (outs[0], outs[1:]) if not end else (None, None)
     arrays, places = gather(got, [f"{step}v" for held in late for step in held])
     places = iter(places)
     v_at = [[next(places) for step in held] for held in late]
     out, top, total = pl.pallas_call(
-        functools.partial(mix_kernel, stages, v_at, kv_heads, group),
+        functools.partial(mix_kernel, carried, v_at, kv_heads, group),
         out_shape=(jax.ShapeDtypeStruct((rows, width), jnp.bfloat16), stat, stat),
         in_specs=[pl.BlockSpec(memory_space=pl.ANY)] * 3 + [VMEM] * (2 * len(stages) + 3 + len(arrays)),
         input_output_aliases={0: 0, 1: 1, 2: 2},

time: 18.2 us -> 18 us (0.989)
  waiting for transfers between devices: 3.28 us -> 2.7 us
  Pallas kernels: 6.18 us -> 6.57 us
    ppermute x2, waiting for transfers between devices: 1.21 us -> 0.62 us  [within(): return lax.ppermute(value, ('outer', 'inner'), pairs)]
    pallas_call x4, Pallas kernels: 6.18 us -> 6.57 us  [the longest x3 4.76 us: body(): pl.pallas_call(functools.partial(weigh_kernel, (order, *stages[1:]) if be...]
  transfers between devices with their start and end apart: 7 -> 7, of which waited for: 3 -> 3; matrix products, arithmetic and copies ran while one was open for 0% -> 0% of each run, Pallas kernels for 23% -> 27%
where the time goes in v5:
time: 18 us; the launch traced here: 17.8 us
  starting transfers between devices  7.76 us (43%)
  Pallas kernels  6.57 us (36%)
  waiting for transfers between devices  2.7 us (15%)
  between operations  0.74 us (4%)
    ppermute x5, starting transfers between devices, direct(): return lax.ppermute(value, ('outer', 'inner'), pairs)  5.72 us
    pallas_call x3, Pallas kernels, body(): pl.pallas_call(functools.partial(weigh_kernel, (order, *stages[1:]) if be...  4.76 us
    ppermute x5, waiting for transfers between devices, direct(): return lax.ppermute(value, ('outer', 'inner'), pairs)  2.08 us
    ppermute x2, starting transfers between devices, within(): return lax.ppermute(value, ('outer', 'inner'), pairs)  2.03 us
    pallas_call x1, Pallas kernels, body(): pl.pallas_call(functools.partial(mix_kernel, carried, v_at, kv_heads, gro...  1.81 us
    ppermute x2, waiting for transfers between devices, within(): return lax.ppermute(value, ('outer', 'inner'), pairs)  0.62 us
  transfers between devices with their start and end apart: 7, of which 3 were waited for; matrix products, arithmetic and copies ran while one was open for 0% of the time, Pallas kernels for 27%

profile of v5, /device:TPU:8, one launch (start us, length us, event | category | flops | bytes accessed | tf_op | source)
XLA Modules:
  0.0 17.8 jit_solution(9051374652897983268)
XLA Ops:
  0.6 1.0 %collective-permute-start.3 = (bf16[128,512]{1,0:T(8,128)(2,1)}, bf16[128,512]{1,0:T(8,128)(2,1)S(1)}, u32[]{:S(2)}, u32[]{:S(2)}) collective-permute-start(bf16[128,512]{1,0:T(8,128)(2,1)} %param.9), channel_id=1, source_target_pairs={{2,4},{3,5},{0,6},{1,7},{6,8},{7,9},{4,10},{5,11},{10,12},{11,13},... | collective-permute-start | bytes 393224 | tf_op jit(solution)/shard_map/ppermute | solution.py:264
  1.6 1.7 %collective-permute-start.5 = (bf16[128,512]{1,0:T(8,128)(2,1)}, bf16[128,512]{1,0:T(8,128)(2,1)S(1)}, u32[]{:S(2)}, u32[]{:S(2)}) collective-permute-start(bf16[128,512]{1,0:T(8,128)(2,1)} %param.9), channel_id=1, source_target_pairs={{0,4},{1,5},{2,6},{3,7},{4,8},{5,9},{6,10},{7,11},{8,12},{9,13},{1... | collective-permute-start | bytes 393224 | tf_op jit(solution)/shard_map/ppermute | solution.py:264
  3.3 1.1 %collective-permute-start.1 = (bf16[128,512]{1,0:T(8,128)(2,1)}, bf16[128,512]{1,0:T(8,128)(2,1)S(1)}, u32[]{:S(2)}, u32[]{:S(2)}) collective-permute-start(bf16[128,512]{1,0:T(8,128)(2,1)} %param.8), channel_id=1, source_target_pairs={{1,4},{0,5},{3,6},{2,7},{5,8},{4,9},{7,10},{6,11},{9,12},{8,13},{1... | collective-permute-start | bytes 393224 | tf_op jit(solution)/shard_map/ppermute | solution.py:264
  4.4 1.5 %collective-permute-start = (bf16[128,512]{1,0:T(8,128)(2,1)}, bf16[128,512]{1,0:T(8,128)(2,1)S(1)}, u32[]{:S(2)}, u32[]{:S(2)}) collective-permute-start(bf16[128,512]{1,0:T(8,128)(2,1)} %param.8), channel_id=1, source_target_pairs={{0,4},{1,5},{2,6},{3,7},{4,8},{5,9},{6,10},{7,11},{8,12},{9,13},{1... | collective-permute-start | bytes 393224 | tf_op jit(solution)/shard_map/ppermute | solution.py:264
  6.0 0.4 %collective-permute-start.2 = (bf16[128,512]{1,0:T(8,128)(2,1)}, bf16[128,512]{1,0:T(8,128)(2,1)S(1)}, u32[]{:S(2)}, u32[]{:S(2)}) collective-permute-start(bf16[128,512]{1,0:T(8,128)(2,1)} %param.8), channel_id=1, source_target_pairs={{2,4},{3,5},{0,6},{1,7},{6,8},{7,9},{4,10},{5,11},{10,12},{11,13},... | collective-permute-start | bytes 393224 | tf_op jit(solution)/shard_map/ppermute | solution.py:264
  6.4 0.0 collective-permute-done.3.refs_7_
  6.4 1.3 %collective-permute-done.5.refs_12_ = bf16[128,512]{1,0:T(8,128)(2,1)S(1)} collective-permute-done((bf16[128,512]{1,0:T(8,128)(2,1)}, bf16[128,512]{1,0:T(8,128)(2,1)S(1)}, u32[]{:S(2)}, u32[]{:S(2)}) %collective-permute-start.5) | collective-permute-done | bytes 131104 | tf_op jit(solution)/shard_map/ppermute | solution.py:264
  7.7 0.0 copy-start
  7.7 0.0 copy-start.1
  7.7 0.0 copy-start.2
  7.8 0.0 copy-start.3
  7.8 0.0 copy-start.4
  7.8 1.6 %collective-permute-start.6 = (bf16[256,512]{1,0:T(8,128)(2,1)S(1)}, bf16[256,512]{1,0:T(8,128)(2,1)S(1)}, u32[]{:S(2)}, u32[]{:S(2)}) collective-permute-start(bf16[256,512]{1,0:T(8,128)(2,1)S(1)} %pad_maximum_fusion), channel_id=1, source_target_pairs={{2,0},{3,1},{0,2},{1,3},{5,4},{4,5},{7,6},{6,7},{9,8},{8,9},{11,10... | collective-permute-start | bytes 786440 | tf_op jit(solution)/shard_map/ppermute | solution.py:270
  9.3 0.7 %collective-permute-done.1.refs_7_ = bf16[128,512]{1,0:T(8,128)(2,1)S(1)} collective-permute-done((bf16[128,512]{1,0:T(8,128)(2,1)}, bf16[128,512]{1,0:T(8,128)(2,1)S(1)}, u32[]{:S(2)}, u32[]{:S(2)}) %collective-permute-start.1) | collective-permute-done | bytes 131104 | tf_op jit(solution)/shard_map/ppermute | solution.py:264
  10.1 0.5 %collective-permute-start.4 = (bf16[128,512]{1,0:T(8,128)(2,1)S(1)}, bf16[128,512]{1,0:T(8,128)(2,1)S(1)}, u32[]{:S(2)}, u32[]{:S(2)}) collective-permute-start(bf16[128,512]{1,0:T(8,128)(2,1)S(1)} %collective-permute-done.1.refs_7_), channel_id=1, source_target_pairs={{1,0},{0,1},{3,2},{2,3},{6,4},{7,5},{4,6},{5,7},{10,8},{11,9},{8,1... | collective-permute-start | bytes 393224 | tf_op jit(solution)/shard_map/ppermute | solution.py:270
  10.5 0.0 collective-permute-done.refs_6_
  10.5 0.0 copy-done
  10.6 0.0 copy-done.1
  10.6 0.0 copy-done.2
  10.6 0.0 copy-done.3
  10.6 0.0 copy-done.4
  10.6 2.4 %shard_map.95 = (bf16[256,4096]{1,0:T(8,128)(2,1)S(1)}, f32[32,128]{1,0:T(8,128)S(1)}, f32[32,128]{1,0:T(8,128)S(1)}, f32[4096,128]{1,0:T(8,128)S(1)}, bf16[128,...) custom-call(s32[16]{0:T(128)S(1)} %copy-done.4, ...), custom_call_target="tpu_custom_call" | custom-call | flops 268435456 | bytes 1048576 | tf_op jit(solution)/shard_map/pallas_call | solution.py:355
  13.0 0.0 collective-permute-done.2.refs_6_
  13.0 1.5 %shard_map.96 = (bf16[128,4096]{1,0:T(8,128)(2,1)S(1)}, f32[32,128]{1,0:T(8,128)S(1)}, f32[32,128]{1,0:T(8,128)S(1)}, f32[32,128]{1,0:T(8,128)S(1)}, f32[4096,128]{1,0:T(8,128)S(1)}) custom-call(bf16[128,128]{1,0:T(8,128)(2,1)S(1)} %get-tuple-element.29.refs_0_, bf16[128,128]{1,0:T(8,128)(2,1)S(1)} %get-tuple-element.31.refs_1_, ...), custom_call_target="tpu_custom_call" | custom-call | flops 268435456 | bytes 1048576 | tf_op jit(solution)/shard_map/pallas_call | solution.py:355
  14.5 0.6 %collective-permute-done.4.refs_5_ = bf16[128,512]{1,0:T(8,128)(2,1)S(1)} collective-permute-done((bf16[128,512]{1,0:T(8,128)(2,1)S(1)}, bf16[128,512]{1,0:T(8,128)(2,1)S(1)}, u32[]{:S(2)}, u32[]{:S(2)}) %collective-permute-start.4) | collective-permute-done | bytes 131104 | tf_op jit(solution)/shard_map/ppermute | solution.py:270
  15.1 0.9 %shard_map.97 = (bf16[128,4096]{1,0:T(8,128)(2,1)S(1)}, f32[32,128]{1,0:T(8,128)S(1)}, f32[32,128]{1,0:T(8,128)S(1)}, f32[32,128]{1,0:T(8,128)S(1)}, f32[32,128]{1,0:T(8,128)S(1)}) custom-call(bf16[128,128]{1,0:T(8,128)(2,1)S(1)} %get-tuple-element.29.refs_0_, bf16[128,128]{1,0:T(8,128)(2,1)S(1)} %get-tuple-element.30.refs_1_, ...), custom_call_target="tpu_custom_call" | custom-call | flops 134217728 | bytes 1048576 | tf_op jit(solution)/shard_map/pallas_call | solution.py:355
  16.0 0.0 collective-permute-done.6.refs_13_
  16.0 1.8 %shard_map.98 = (bf16[128,4096]{1,0:T(8,128)(2,1)}, f32[32,128]{1,0:T(8,128)}, f32[32,128]{1,0:T(8,128)}) custom-call(bf16[128,4096]{1,0:T(8,128)(2,1)} %get-tuple-element.26.refs_0_, f32[32,128]{1,0:T(8,128)} %get-tuple-element.27.refs_1_, f32[32,128]{1,0:T(8,128)} %get-tuple-element.28.refs_2_, ...), custom_call_target="tpu_custom_call", output_to_operand_aliasing={{0}: (0, {}), {1}: (1, {}), {2}: (2, {})} | custom-call | flops 536870912 | bytes 1048576 | tf_op jit(solution)/shard_map/pallas_call | solution.py:395
  (2 shorter events, 0.0 us)
Async XLA Ops:
  0.6 5.7 %collective-permute-start.3 = (bf16[128,512]{1,0:T(8,128)(2,1)}, bf16[128,512]{1,0:T(8,128)(2,1)S(1)}, u32[]{:S(2)}, u32[]{:S(2)}) collective-permute-start(bf16[128,512]{1,0:T(8,128)(2,1)} %param.9), channel_id=1, source_target_pairs={{2,4},{3,5},{0,6},{1,7},{6,8},{7,9},{4,10},{5,11},{10,12},{11,13},... | collective-permute-start | bytes 393224 | tf_op jit(solution)/shard_map/ppermute | solution.py:264
  1.6 6.1 %collective-permute-start.5 = (bf16[128,512]{1,0:T(8,128)(2,1)}, bf16[128,512]{1,0:T(8,128)(2,1)S(1)}, u32[]{:S(2)}, u32[]{:S(2)}) collective-permute-start(bf16[128,512]{1,0:T(8,128)(2,1)} %param.9), channel_id=1, source_target_pairs={{0,4},{1,5},{2,6},{3,7},{4,8},{5,9},{6,10},{7,11},{8,12},{9,13},{1... | collective-permute-start | bytes 393224 | tf_op jit(solution)/shard_map/ppermute | solution.py:264
  3.3 6.7 %collective-permute-start.1 = (bf16[128,512]{1,0:T(8,128)(2,1)}, bf16[128,512]{1,0:T(8,128)(2,1)S(1)}, u32[]{:S(2)}, u32[]{:S(2)}) collective-permute-start(bf16[128,512]{1,0:T(8,128)(2,1)} %param.8), channel_id=1, source_target_pairs={{1,4},{0,5},{3,6},{2,7},{5,8},{4,9},{7,10},{6,11},{9,12},{8,13},{1... | collective-permute-start | bytes 393224 | tf_op jit(solution)/shard_map/ppermute | solution.py:264
  4.4 6.1 %collective-permute-start = (bf16[128,512]{1,0:T(8,128)(2,1)}, bf16[128,512]{1,0:T(8,128)(2,1)S(1)}, u32[]{:S(2)}, u32[]{:S(2)}) collective-permute-start(bf16[128,512]{1,0:T(8,128)(2,1)} %param.8), channel_id=1, source_target_pairs={{0,4},{1,5},{2,6},{3,7},{4,8},{5,9},{6,10},{7,11},{8,12},{9,13},{1... | collective-permute-start | bytes 393224 | tf_op jit(solution)/shard_map/ppermute | solution.py:264
  6.0 7.1 %collective-permute-start.2 = (bf16[128,512]{1,0:T(8,128)(2,1)}, bf16[128,512]{1,0:T(8,128)(2,1)S(1)}, u32[]{:S(2)}, u32[]{:S(2)}) collective-permute-start(bf16[128,512]{1,0:T(8,128)(2,1)} %param.8), channel_id=1, source_target_pairs={{2,4},{3,5},{0,6},{1,7},{6,8},{7,9},{4,10},{5,11},{10,12},{11,13},... | collective-permute-start | bytes 393224 | tf_op jit(solution)/shard_map/ppermute | solution.py:264
  7.7 2.8 %copy-start = (bf16[128,4096]{1,0:T(8,128)(2,1)S(1)}, bf16[128,4096]{1,0:T(8,128)(2,1)}, u32[]{:S(2)}) copy-start(bf16[128,4096]{1,0:T(8,128)(2,1)} %refs_2_.3) | copy-start | bytes 3145732
  7.7 2.8 %copy-start.1 = (bf16[128,4096]{1,0:T(8,128)(2,1)S(1)}, bf16[128,4096]{1,0:T(8,128)(2,1)}, u32[]{:S(2)}) copy-start(bf16[128,4096]{1,0:T(8,128)(2,1)} %refs_2_.2) | copy-start | bytes 3145732
  7.7 2.8 %copy-start.2 = (f32[128,32]{0,1:T(8,128)S(1)}, f32[128,32]{0,1:T(8,128)}, u32[]{:S(2)}) copy-start(f32[128,32]{0,1:T(8,128)} %param.11) | copy-start | bytes 49156
  7.8 2.8 %copy-start.3 = (f32[128,32]{0,1:T(8,128)S(1)}, f32[128,32]{0,1:T(8,128)}, u32[]{:S(2)}) copy-start(f32[128,32]{0,1:T(8,128)} %param.12) | copy-start | bytes 49156
  7.8 2.8 %copy-start.4 = (s32[16]{0:T(128)S(1)}, s32[16]{0:T(128)}, u32[]{:S(2)}) copy-start(s32[16]{0:T(128)} %refs_0_.1) | copy-start | bytes 196
  7.8 8.2 %collective-permute-start.6 = (bf16[256,512]{1,0:T(8,128)(2,1)S(1)}, bf16[256,512]{1,0:T(8,128)(2,1)S(1)}, u32[]{:S(2)}, u32[]{:S(2)}) collective-permute-start(bf16[256,512]{1,0:T(8,128)(2,1)S(1)} %pad_maximum_fusion), channel_id=1, source_target_pairs={{2,0},{3,1},{0,2},{1,3},{5,4},{4,5},{7,6},{6,7},{9,8},{8,9},{11,10... | collective-permute-start | bytes 786440 | tf_op jit(solution)/shard_map/ppermute | solution.py:270
  10.1 5.1 %collective-permute-start.4 = (bf16[128,512]{1,0:T(8,128)(2,1)S(1)}, bf16[128,512]{1,0:T(8,128)(2,1)S(1)}, u32[]{:S(2)}, u32[]{:S(2)}) collective-permute-start(bf16[128,512]{1,0:T(8,128)(2,1)S(1)} %collective-permute-done.1.refs_7_), channel_id=1, source_target_pairs={{1,0},{0,1},{3,2},{2,3},{6,4},{7,5},{4,6},{5,7},{10,8},{11,9},{8,1... | collective-permute-start | bytes 393224 | tf_op jit(solution)/shard_map/ppermute | solution.py:270

commit v6 on v5

--- a/solution.py
+++ b/solution.py
@@ -373,7 +373,7 @@
             else [],
             compiler_params=pltpu.CompilerParams(vmem_limit_bytes=12 * 2**20),
             cost_estimate=pl.CostEstimate(
-                flops=2 * area * HD * (len(steps) + len(now)), bytes_accessed=2**20, transcendentals=area * len(steps)
+                flops=8 * area * HD * (len(steps) + len(now)), bytes_accessed=2**20, transcendentals=area * len(steps)
             ),
         )(*operands)
         outs = list(outs)

time: 18 us -> 17.8 us (0.989)
  no operation moved by 1% of the time
where the time goes in v6:
time: 17.8 us; the launch traced here: 17.7 us
  starting transfers between devices  7.76 us (44%)
  Pallas kernels  6.44 us (36%)
  waiting for transfers between devices  2.71 us (15%)
  between operations  0.74 us (4%)
    ppermute x5, starting transfers between devices, direct(): return lax.ppermute(value, ('outer', 'inner'), pairs)  5.72 us
    pallas_call x3, Pallas kernels, body(): pl.pallas_call(functools.partial(weigh_kernel, (order, *stages[1:]) if be...  4.73 us
    ppermute x5, waiting for transfers between devices, direct(): return lax.ppermute(value, ('outer', 'inner'), pairs)  2.08 us
    ppermute x2, starting transfers between devices, within(): return lax.ppermute(value, ('outer', 'inner'), pairs)  2.03 us
    pallas_call x1, Pallas kernels, body(): pl.pallas_call(functools.partial(mix_kernel, carried, v_at, kv_heads, gro...  1.71 us
    ppermute x2, waiting for transfers between devices, within(): return lax.ppermute(value, ('outer', 'inner'), pairs)  0.63 us
  transfers between devices with their start and end apart: 7, of which 3 were waited for; matrix products, arithmetic and copies ran while one was open for 0% of the time, Pallas kernels for 27%

profile of v6, /device:TPU:8, one launch (start us, length us, event | category | flops | bytes accessed | tf_op | source)
XLA Modules:
  0.0 17.7 jit_solution(5319321398499805253)
XLA Ops:
  0.6 1.0 %collective-permute-start.3 = (bf16[128,512]{1,0:T(8,128)(2,1)}, bf16[128,512]{1,0:T(8,128)(2,1)S(1)}, u32[]{:S(2)}, u32[]{:S(2)}) collective-permute-start(bf16[128,512]{1,0:T(8,128)(2,1)} %param.9), channel_id=1, source_target_pairs={{2,4},{3,5},{0,6},{1,7},{6,8},{7,9},{4,10},{5,11},{10,12},{11,13},... | collective-permute-start | bytes 393224 | tf_op jit(solution)/shard_map/ppermute | solution.py:264
  1.6 1.7 %collective-permute-start.5 = (bf16[128,512]{1,0:T(8,128)(2,1)}, bf16[128,512]{1,0:T(8,128)(2,1)S(1)}, u32[]{:S(2)}, u32[]{:S(2)}) collective-permute-start(bf16[128,512]{1,0:T(8,128)(2,1)} %param.9), channel_id=1, source_target_pairs={{0,4},{1,5},{2,6},{3,7},{4,8},{5,9},{6,10},{7,11},{8,12},{9,13},{1... | collective-permute-start | bytes 393224 | tf_op jit(solution)/shard_map/ppermute | solution.py:264
  3.3 1.1 %collective-permute-start.1 = (bf16[128,512]{1,0:T(8,128)(2,1)}, bf16[128,512]{1,0:T(8,128)(2,1)S(1)}, u32[]{:S(2)}, u32[]{:S(2)}) collective-permute-start(bf16[128,512]{1,0:T(8,128)(2,1)} %param.8), channel_id=1, source_target_pairs={{1,4},{0,5},{3,6},{2,7},{5,8},{4,9},{7,10},{6,11},{9,12},{8,13},{1... | collective-permute-start | bytes 393224 | tf_op jit(solution)/shard_map/ppermute | solution.py:264
  4.4 1.5 %collective-permute-start = (bf16[128,512]{1,0:T(8,128)(2,1)}, bf16[128,512]{1,0:T(8,128)(2,1)S(1)}, u32[]{:S(2)}, u32[]{:S(2)}) collective-permute-start(bf16[128,512]{1,0:T(8,128)(2,1)} %param.8), channel_id=1, source_target_pairs={{0,4},{1,5},{2,6},{3,7},{4,8},{5,9},{6,10},{7,11},{8,12},{9,13},{1... | collective-permute-start | bytes 393224 | tf_op jit(solution)/shard_map/ppermute | solution.py:264
  6.0 0.4 %collective-permute-start.2 = (bf16[128,512]{1,0:T(8,128)(2,1)}, bf16[128,512]{1,0:T(8,128)(2,1)S(1)}, u32[]{:S(2)}, u32[]{:S(2)}) collective-permute-start(bf16[128,512]{1,0:T(8,128)(2,1)} %param.8), channel_id=1, source_target_pairs={{2,4},{3,5},{0,6},{1,7},{6,8},{7,9},{4,10},{5,11},{10,12},{11,13},... | collective-permute-start | bytes 393224 | tf_op jit(solution)/shard_map/ppermute | solution.py:264
  6.4 0.0 collective-permute-done.3.refs_7_
  6.4 1.3 %collective-permute-done.5.refs_12_ = bf16[128,512]{1,0:T(8,128)(2,1)S(1)} collective-permute-done((bf16[128,512]{1,0:T(8,128)(2,1)}, bf16[128,512]{1,0:T(8,128)(2,1)S(1)}, u32[]{:S(2)}, u32[]{:S(2)}) %collective-permute-start.5) | collective-permute-done | bytes 131104 | tf_op jit(solution)/shard_map/ppermute | solution.py:264
  7.7 0.0 copy-start
  7.7 0.0 copy-start.1
  7.7 0.0 copy-start.2
  7.8 0.0 copy-start.3
  7.8 0.0 copy-start.4
  7.8 1.6 %collective-permute-start.6 = (bf16[256,512]{1,0:T(8,128)(2,1)S(1)}, bf16[256,512]{1,0:T(8,128)(2,1)S(1)}, u32[]{:S(2)}, u32[]{:S(2)}) collective-permute-start(bf16[256,512]{1,0:T(8,128)(2,1)S(1)} %pad_maximum_fusion), channel_id=1, source_target_pairs={{2,0},{3,1},{0,2},{1,3},{5,4},{4,5},{7,6},{6,7},{9,8},{8,9},{11,10... | collective-permute-start | bytes 786440 | tf_op jit(solution)/shard_map/ppermute | solution.py:270
  9.3 0.7 %collective-permute-done.1.refs_7_ = bf16[128,512]{1,0:T(8,128)(2,1)S(1)} collective-permute-done((bf16[128,512]{1,0:T(8,128)(2,1)}, bf16[128,512]{1,0:T(8,128)(2,1)S(1)}, u32[]{:S(2)}, u32[]{:S(2)}) %collective-permute-start.1) | collective-permute-done | bytes 131104 | tf_op jit(solution)/shard_map/ppermute | solution.py:264
  10.1 0.5 %collective-permute-start.4 = (bf16[128,512]{1,0:T(8,128)(2,1)S(1)}, bf16[128,512]{1,0:T(8,128)(2,1)S(1)}, u32[]{:S(2)}, u32[]{:S(2)}) collective-permute-start(bf16[128,512]{1,0:T(8,128)(2,1)S(1)} %collective-permute-done.1.refs_7_), channel_id=1, source_target_pairs={{1,0},{0,1},{3,2},{2,3},{6,4},{7,5},{4,6},{5,7},{10,8},{11,9},{8,1... | collective-permute-start | bytes 393224 | tf_op jit(solution)/shard_map/ppermute | solution.py:270
  10.5 0.0 collective-permute-done.refs_6_
  10.5 0.0 copy-done
  10.6 0.0 copy-done.1
  10.6 0.0 copy-done.2
  10.6 0.0 copy-done.3
  10.6 0.0 copy-done.4
  10.6 2.4 %shard_map.95 = (bf16[256,4096]{1,0:T(8,128)(2,1)S(1)}, f32[32,128]{1,0:T(8,128)S(1)}, f32[32,128]{1,0:T(8,128)S(1)}, f32[4096,128]{1,0:T(8,128)S(1)}, bf16[128,...) custom-call(s32[16]{0:T(128)S(1)} %copy-done.4, ...), custom_call_target="tpu_custom_call" | custom-call | flops 1073741824 | bytes 1048576 | tf_op jit(solution)/shard_map/pallas_call | solution.py:355
  13.0 0.0 collective-permute-done.2.refs_6_
  13.0 1.5 %shard_map.96 = (bf16[128,4096]{1,0:T(8,128)(2,1)S(1)}, f32[32,128]{1,0:T(8,128)S(1)}, f32[32,128]{1,0:T(8,128)S(1)}, f32[32,128]{1,0:T(8,128)S(1)}, f32[4096,128]{1,0:T(8,128)S(1)}) custom-call(bf16[128,128]{1,0:T(8,128)(2,1)S(1)} %get-tuple-element.29.refs_0_, bf16[128,128]{1,0:T(8,128)(2,1)S(1)} %get-tuple-element.31.refs_1_, ...), custom_call_target="tpu_custom_call" | custom-call | flops 1073741824 | bytes 1048576 | tf_op jit(solution)/shard_map/pallas_call | solution.py:355
  14.5 0.6 %collective-permute-done.4.refs_5_ = bf16[128,512]{1,0:T(8,128)(2,1)S(1)} collective-permute-done((bf16[128,512]{1,0:T(8,128)(2,1)S(1)}, bf16[128,512]{1,0:T(8,128)(2,1)S(1)}, u32[]{:S(2)}, u32[]{:S(2)}) %collective-permute-start.4) | collective-permute-done | bytes 131104 | tf_op jit(solution)/shard_map/ppermute | solution.py:270
  15.1 0.8 %shard_map.97 = (bf16[128,4096]{1,0:T(8,128)(2,1)S(1)}, f32[32,128]{1,0:T(8,128)S(1)}, f32[32,128]{1,0:T(8,128)S(1)}, f32[32,128]{1,0:T(8,128)S(1)}, f32[32,128]{1,0:T(8,128)S(1)}) custom-call(bf16[128,128]{1,0:T(8,128)(2,1)S(1)} %get-tuple-element.29.refs_0_, bf16[128,128]{1,0:T(8,128)(2,1)S(1)} %get-tuple-element.30.refs_1_, ...), custom_call_target="tpu_custom_call" | custom-call | flops 536870912 | bytes 1048576 | tf_op jit(solution)/shard_map/pallas_call | solution.py:355
  16.0 0.0 collective-permute-done.6.refs_13_
  16.0 1.7 %shard_map.98 = (bf16[128,4096]{1,0:T(8,128)(2,1)}, f32[32,128]{1,0:T(8,128)}, f32[32,128]{1,0:T(8,128)}) custom-call(bf16[128,4096]{1,0:T(8,128)(2,1)} %get-tuple-element.26.refs_0_, f32[32,128]{1,0:T(8,128)} %get-tuple-element.27.refs_1_, f32[32,128]{1,0:T(8,128)} %get-tuple-element.28.refs_2_, ...), custom_call_target="tpu_custom_call", output_to_operand_aliasing={{0}: (0, {}), {1}: (1, {}), {2}: (2, {})} | custom-call | flops 536870912 | bytes 1048576 | tf_op jit(solution)/shard_map/pallas_call | solution.py:395
  (2 shorter events, 0.0 us)
Async XLA Ops:
  0.6 5.7 %collective-permute-start.3 = (bf16[128,512]{1,0:T(8,128)(2,1)}, bf16[128,512]{1,0:T(8,128)(2,1)S(1)}, u32[]{:S(2)}, u32[]{:S(2)}) collective-permute-start(bf16[128,512]{1,0:T(8,128)(2,1)} %param.9), channel_id=1, source_target_pairs={{2,4},{3,5},{0,6},{1,7},{6,8},{7,9},{4,10},{5,11},{10,12},{11,13},... | collective-permute-start | bytes 393224 | tf_op jit(solution)/shard_map/ppermute | solution.py:264
  1.6 6.1 %collective-permute-start.5 = (bf16[128,512]{1,0:T(8,128)(2,1)}, bf16[128,512]{1,0:T(8,128)(2,1)S(1)}, u32[]{:S(2)}, u32[]{:S(2)}) collective-permute-start(bf16[128,512]{1,0:T(8,128)(2,1)} %param.9), channel_id=1, source_target_pairs={{0,4},{1,5},{2,6},{3,7},{4,8},{5,9},{6,10},{7,11},{8,12},{9,13},{1... | collective-permute-start | bytes 393224 | tf_op jit(solution)/shard_map/ppermute | solution.py:264
  3.3 6.7 %collective-permute-start.1 = (bf16[128,512]{1,0:T(8,128)(2,1)}, bf16[128,512]{1,0:T(8,128)(2,1)S(1)}, u32[]{:S(2)}, u32[]{:S(2)}) collective-permute-start(bf16[128,512]{1,0:T(8,128)(2,1)} %param.8), channel_id=1, source_target_pairs={{1,4},{0,5},{3,6},{2,7},{5,8},{4,9},{7,10},{6,11},{9,12},{8,13},{1... | collective-permute-start | bytes 393224 | tf_op jit(solution)/shard_map/ppermute | solution.py:264
  4.4 6.1 %collective-permute-start = (bf16[128,512]{1,0:T(8,128)(2,1)}, bf16[128,512]{1,0:T(8,128)(2,1)S(1)}, u32[]{:S(2)}, u32[]{:S(2)}) collective-permute-start(bf16[128,512]{1,0:T(8,128)(2,1)} %param.8), channel_id=1, source_target_pairs={{0,4},{1,5},{2,6},{3,7},{4,8},{5,9},{6,10},{7,11},{8,12},{9,13},{1... | collective-permute-start | bytes 393224 | tf_op jit(solution)/shard_map/ppermute | solution.py:264
  6.0 7.1 %collective-permute-start.2 = (bf16[128,512]{1,0:T(8,128)(2,1)}, bf16[128,512]{1,0:T(8,128)(2,1)S(1)}, u32[]{:S(2)}, u32[]{:S(2)}) collective-permute-start(bf16[128,512]{1,0:T(8,128)(2,1)} %param.8), channel_id=1, source_target_pairs={{2,4},{3,5},{0,6},{1,7},{6,8},{7,9},{4,10},{5,11},{10,12},{11,13},... | collective-permute-start | bytes 393224 | tf_op jit(solution)/shard_map/ppermute | solution.py:264
  7.7 2.8 %copy-start = (bf16[128,4096]{1,0:T(8,128)(2,1)S(1)}, bf16[128,4096]{1,0:T(8,128)(2,1)}, u32[]{:S(2)}) copy-start(bf16[128,4096]{1,0:T(8,128)(2,1)} %refs_2_.2) | copy-start | bytes 3145732
  7.7 2.8 %copy-start.1 = (bf16[128,4096]{1,0:T(8,128)(2,1)S(1)}, bf16[128,4096]{1,0:T(8,128)(2,1)}, u32[]{:S(2)}) copy-start(bf16[128,4096]{1,0:T(8,128)(2,1)} %refs_2_.3) | copy-start | bytes 3145732
  7.7 2.8 %copy-start.2 = (f32[128,32]{0,1:T(8,128)S(1)}, f32[128,32]{0,1:T(8,128)}, u32[]{:S(2)}) copy-start(f32[128,32]{0,1:T(8,128)} %param.11) | copy-start | bytes 49156
  7.8 2.8 %copy-start.3 = (f32[128,32]{0,1:T(8,128)S(1)}, f32[128,32]{0,1:T(8,128)}, u32[]{:S(2)}) copy-start(f32[128,32]{0,1:T(8,128)} %param.12) | copy-start | bytes 49156
  7.8 2.8 %copy-start.4 = (s32[16]{0:T(128)S(1)}, s32[16]{0:T(128)}, u32[]{:S(2)}) copy-start(s32[16]{0:T(128)} %refs_0_.1) | copy-start | bytes 196
  7.8 8.2 %collective-permute-start.6 = (bf16[256,512]{1,0:T(8,128)(2,1)S(1)}, bf16[256,512]{1,0:T(8,128)(2,1)S(1)}, u32[]{:S(2)}, u32[]{:S(2)}) collective-permute-start(bf16[256,512]{1,0:T(8,128)(2,1)S(1)} %pad_maximum_fusion), channel_id=1, source_target_pairs={{2,0},{3,1},{0,2},{1,3},{5,4},{4,5},{7,6},{6,7},{9,8},{8,9},{11,10... | collective-permute-start | bytes 786440 | tf_op jit(solution)/shard_map/ppermute | solution.py:270
  10.1 5.1 %collective-permute-start.4 = (bf16[128,512]{1,0:T(8,128)(2,1)S(1)}, bf16[128,512]{1,0:T(8,128)(2,1)S(1)}, u32[]{:S(2)}, u32[]{:S(2)}) collective-permute-start(bf16[128,512]{1,0:T(8,128)(2,1)S(1)} %collective-permute-done.1.refs_7_), channel_id=1, source_target_pairs={{1,0},{0,1},{3,2},{2,3},{6,4},{7,5},{4,6},{5,7},{10,8},{11,9},{8,1... | collective-permute-start | bytes 393224 | tf_op jit(solution)/shard_map/ppermute | solution.py:270
